TPU v7x, 32 devices: a whole 2x2x4 slice. The times are simulated.
32 devices in a mesh: grp: 8 (over z, x), seq: 4 (over y, core).
Axes of the slice: x: 2, y: 2, z: 4, core: 2. Of those that a mesh axis runs over, the one named last changes fastest.
Arguments:
- tokens: bfloat16 [16, 448, 768], P('grp', 'seq'), may hold values from -6 to 6
- encoder_states: bfloat16 [16, 1500, 768], P('grp', 'seq'), may hold values from -6 to 6
- lengths: int32 [16], P('grp'), may hold values from 56 to 448, as said below
- frame_counts: int32 [16], P('grp'), may hold values from 375 to 1500, as said below
- corpus_ids: int32 [16], P('grp'), may hold values from 0 to 8
- corpus_weights: float32 [9], replicated, may hold values from 0.5 to 2
- cotangent: bfloat16 [16, 448, 768], P('grp', 'seq'), may hold values from -6 to 6
- first_gain: bfloat16 [768], P('grp'), may hold values from 0.5 to 1.5
- first_bias: bfloat16 [768], P('grp'), may hold values from -1.5 to 1.5
- query_weight: bfloat16 [768, 768], P('grp', 'seq'), may hold values from -0.3125 to 0.3125
- query_bias: bfloat16 [768], P('grp'), may hold values from -1.5 to 1.5
- key_weight: bfloat16 [768, 768], P('grp', 'seq'), may hold values from -0.3125 to 0.3125
- value_weight: bfloat16 [768, 768], P('grp', 'seq'), may hold values from -0.21875 to 0.21875
- value_bias: bfloat16 [768], P('grp'), may hold values from -1.5 to 1.5
- output_weight: bfloat16 [768, 768], P('grp', 'seq'), may hold values from -1.75 to 1.75
- output_bias: bfloat16 [768], P('grp'), may hold values from -1.5 to 1.5
- second_gain: bfloat16 [768], P('grp'), may hold values from 0.5 to 1.5
- second_bias: bfloat16 [768], P('grp'), may hold values from -1.5 to 1.5
- cross_query_weight: bfloat16 [768, 768], P('grp', 'seq'), may hold values from -0.3125 to 0.3125
- cross_query_bias: bfloat16 [768], P('grp'), may hold values from -1.5 to 1.5
- cross_key_weight: bfloat16 [768, 768], P('grp', 'seq'), may hold values from -0.3125 to 0.3125
- cross_value_weight: bfloat16 [768, 768], P('grp', 'seq'), may hold values from -0.21875 to 0.21875
- cross_value_bias: bfloat16 [768], P('grp'), may hold values from -1.5 to 1.5
- cross_output_weight: bfloat16 [768, 768], P('grp', 'seq'), may hold values from -2.5 to 2.5
- cross_output_bias: bfloat16 [768], P('grp'), may hold values from -1.5 to 1.5
- third_gain: bfloat16 [768], P('grp'), may hold values from 0.5 to 1.5
- third_bias: bfloat16 [768], P('grp'), may hold values from -1.5 to 1.5
- expand_weight: bfloat16 [768, 3072], P('grp', 'seq'), may hold values from -0.21875 to 0.21875
- expand_bias: bfloat16 [3072], P('grp'), may hold values from -1.5 to 1.5
- reduce_weight: bfloat16 [3072, 768], P('grp', 'seq'), may hold values from -0.109375 to 0.109375
- reduce_bias: bfloat16 [768], P('grp'), may hold values from -1.5 to 1.5
Outputs:
- layer_output: bfloat16 [16, 448, 768], P('grp', 'seq')
- tokens_gradient: bfloat16 [16, 448, 768], P('grp', 'seq')
- first_gain_gradient: float32 [768], P('grp')
- first_bias_gradient: float32 [768], P('grp')
- query_weight_gradient: float32 [768, 768], P('grp', 'seq')
- query_bias_gradient: float32 [768], P('grp')
- key_weight_gradient: float32 [768, 768], P('grp', 'seq')
- value_weight_gradient: float32 [768, 768], P('grp', 'seq')
- value_bias_gradient: float32 [768], P('grp')
- output_weight_gradient: float32 [768, 768], P('grp', 'seq')
- output_bias_gradient: float32 [768], P('grp')
- second_gain_gradient: float32 [768], P('grp')
- second_bias_gradient: float32 [768], P('grp')
- cross_query_weight_gradient: float32 [768, 768], P('grp', 'seq')
- cross_query_bias_gradient: float32 [768], P('grp')
- cross_key_weight_gradient: float32 [768, 768], P('grp', 'seq')
- cross_value_weight_gradient: float32 [768, 768], P('grp', 'seq')
- cross_value_bias_gradient: float32 [768], P('grp')
- cross_output_weight_gradient: float32 [768, 768], P('grp', 'seq')
- cross_output_bias_gradient: float32 [768], P('grp')
- third_gain_gradient: float32 [768], P('grp')
- third_bias_gradient: float32 [768], P('grp')
- expand_weight_gradient: float32 [768, 3072], P('grp', 'seq')
- expand_bias_gradient: float32 [3072], P('grp')
- reduce_weight_gradient: float32 [3072, 768], P('grp', 'seq')
- reduce_bias_gradient: float32 [768], P('grp')
Inputs may be any that keep to these rules, and one draw needn't show every extreme that they name: `lengths`: in each aligned block of 2 transcripts one has more than 336 valid tokens; some transcript has exactly 448. `frame_counts`: in each aligned block of 2 clips one has more than 1125 valid frames; some clip has exactly 1500.
All inputs are finite; a program needn't handle non-finite values.
Results may differ from a plain program's by a relative error of at most 0.025.
Values may be sent and summed in bfloat16 or wider, within the bound.
A program may use at most 192 MiB of HBM per device.

v0:
```python
import math

import jax
import jax.numpy as jnp
from jax import lax
from jax.experimental import pallas as pl
from jax.experimental.pallas import tpu as pltpu
from jax.sharding import PartitionSpec as P

HEADS = 12
HEAD_DIM = 64


NEG = -1e30
EPS = 1e-05


def norm_rows(values, scaling, offset):
    centre = values - jnp.mean(values, axis=-1, keepdims=True)
    spread = jnp.mean(centre * centre, axis=-1, keepdims=True)
    return centre * lax.rsqrt(spread + EPS) * scaling + offset


def smooth_gate(values):
    return 0.5 * values * (1.0 + lax.erf(values * 0.7071067811865476))


def linear(inputs, weight):
    return jnp.einsum("bri,ij->brj", inputs, weight, preferred_element_type=jnp.float32)


def linear_back(gradient, weight):
    return jnp.einsum("brj,ij->bri", gradient, weight, preferred_element_type=jnp.float32)


def outer_sum(inputs, gradient):
    return jnp.einsum("bri,brj->ij", inputs, gradient, preferred_element_type=jnp.float32)


def row_total(gradient):
    return jnp.sum(gradient.astype(jnp.float32), axis=(0, 1))


def split_heads(values):
    return values.reshape(values.shape[0], values.shape[1], HEADS, HEAD_DIM)


def scores_of(query, key_rows, allowed):
    scores = jnp.einsum(
        "bqhd,bkhd->bhqk",
        split_heads(query),
        split_heads(key_rows),
        preferred_element_type=jnp.float32,
    )
    return jnp.where(allowed[:, None], scores, NEG)


def attend(query, key_rows, values, allowed):
    scores = scores_of(query, key_rows, allowed)
    maximum = jnp.max(scores, axis=-1, keepdims=True)
    raised = jnp.exp(scores - maximum)
    summed = jnp.sum(raised, axis=-1, keepdims=True)
    chances = (raised / summed).astype(jnp.bfloat16)
    blended = jnp.einsum(
        "bhqk,bkhd->bqhd", chances, split_heads(values), preferred_element_type=jnp.float32
    )
    return (blended.reshape(query.shape).astype(jnp.bfloat16), maximum + jnp.log(summed))


def attend_back(grad_low, query, key_rows, values, allowed, logsum):
    scores = scores_of(query, key_rows, allowed)
    chances = jnp.exp(scores - logsum)
    grad_heads = split_heads(grad_low)
    grad_chance = jnp.einsum(
        "bqhd,bkhd->bhqk", grad_heads, split_heads(values), preferred_element_type=jnp.float32
    )
    offset = jnp.sum(chances * grad_chance, axis=-1, keepdims=True)
    grad_score = (chances * (grad_chance - offset)).astype(jnp.bfloat16)
    grad_query = jnp.einsum(
        "bhqk,bkhd->bqhd", grad_score, split_heads(key_rows), preferred_element_type=jnp.float32
    )
    grad_keys = jnp.einsum(
        "bhqk,bqhd->bkhd", grad_score, split_heads(query), preferred_element_type=jnp.float32
    )
    grad_values = jnp.einsum(
        "bhqk,bqhd->bkhd",
        chances.astype(jnp.bfloat16),
        grad_heads,
        preferred_element_type=jnp.float32,
    )
    return (
        grad_query.reshape(query.shape),
        grad_keys.reshape(key_rows.shape),
        grad_values.reshape(values.shape),
    )


def on_device_plain(
    tokens,
    encoder_states,
    lengths,
    frame_counts,
    corpus_ids,
    corpus_weights,
    cotangent,
    first_gain,
    first_bias,
    query_weight,
    query_bias,
    key_weight,
    value_weight,
    value_bias,
    output_weight,
    output_bias,
    second_gain,
    second_bias,
    cross_query_weight,
    cross_query_bias,
    cross_key_weight,
    cross_value_weight,
    cross_value_bias,
    cross_output_weight,
    cross_output_bias,
    third_gain,
    third_bias,
    expand_weight,
    expand_bias,
    reduce_weight,
    reduce_bias,
):
    row_parts = (
        lax.all_gather(query_weight, "grp", axis=0, tiled=True),
        lax.all_gather(key_weight, "grp", axis=0, tiled=True),
        lax.all_gather(value_weight, "grp", axis=0, tiled=True),
        lax.all_gather(output_weight, "grp", axis=0, tiled=True),
        lax.all_gather(cross_query_weight, "grp", axis=0, tiled=True),
        lax.all_gather(cross_key_weight, "grp", axis=0, tiled=True),
        lax.all_gather(cross_value_weight, "grp", axis=0, tiled=True),
        lax.all_gather(cross_output_weight, "grp", axis=0, tiled=True),
        lax.all_gather(expand_weight, "grp", axis=0, tiled=True),
        lax.all_gather(reduce_weight, "grp", axis=0, tiled=True),
        lax.all_gather(first_gain, "grp", axis=0, tiled=True),
        lax.all_gather(first_bias, "grp", axis=0, tiled=True),
        lax.all_gather(query_bias, "grp", axis=0, tiled=True),
        lax.all_gather(value_bias, "grp", axis=0, tiled=True),
        lax.all_gather(output_bias, "grp", axis=0, tiled=True),
        lax.all_gather(second_gain, "grp", axis=0, tiled=True),
        lax.all_gather(second_bias, "grp", axis=0, tiled=True),
        lax.all_gather(cross_query_bias, "grp", axis=0, tiled=True),
        lax.all_gather(cross_value_bias, "grp", axis=0, tiled=True),
        lax.all_gather(cross_output_bias, "grp", axis=0, tiled=True),
        lax.all_gather(third_gain, "grp", axis=0, tiled=True),
        lax.all_gather(third_bias, "grp", axis=0, tiled=True),
        lax.all_gather(expand_bias, "grp", axis=0, tiled=True),
        lax.all_gather(reduce_bias, "grp", axis=0, tiled=True),
    )
    gathered = (
        lax.all_gather(row_parts[0], "seq", axis=1, tiled=True),
        lax.all_gather(row_parts[1], "seq", axis=1, tiled=True),
        lax.all_gather(row_parts[2], "seq", axis=1, tiled=True),
        lax.all_gather(row_parts[3], "seq", axis=1, tiled=True),
        lax.all_gather(row_parts[4], "seq", axis=1, tiled=True),
        lax.all_gather(row_parts[5], "seq", axis=1, tiled=True),
        lax.all_gather(row_parts[6], "seq", axis=1, tiled=True),
        lax.all_gather(row_parts[7], "seq", axis=1, tiled=True),
        lax.all_gather(row_parts[8], "seq", axis=1, tiled=True),
        lax.all_gather(row_parts[9], "seq", axis=1, tiled=True),
    )
    w_query, w_key, w_value, w_mixer, x_query, x_key, x_value, x_mixer, w_expand, w_reduce = (
        gathered
    )
    vectors = [piece.astype(jnp.float32) for piece in row_parts[10:]]
    factor = 1.0 / math.sqrt(HEAD_DIM)
    seq_count = lax.axis_size("seq")
    span_rows = tokens.shape[1]
    query_pos = lax.axis_index("seq") * span_rows + jnp.arange(span_rows, dtype=jnp.int32)
    key_pos = jnp.arange(span_rows * seq_count, dtype=jnp.int32)
    self_mask = (key_pos[None, None, :] <= query_pos[None, :, None]) & (
        key_pos[None, None, :] < lengths[:, None, None]
    )
    frame_pos = jnp.arange(encoder_states.shape[1] * seq_count, dtype=jnp.int32)
    cross_mask = frame_pos[None, None, :] < frame_counts[:, None, None]
    layer_in = tokens.astype(jnp.float32)
    normed_one, norm_back_one = jax.vjp(norm_rows, layer_in, vectors[0], vectors[1])
    normed_one = normed_one.astype(jnp.bfloat16)
    query_low = ((linear(normed_one, w_query) + vectors[2]) * factor).astype(jnp.bfloat16)
    key_low = linear(normed_one, w_key).astype(jnp.bfloat16)
    value_low = (linear(normed_one, w_value) + vectors[3]).astype(jnp.bfloat16)
    key_all, value_all = (
        lax.all_gather(key_low, "seq", axis=1, tiled=True),
        lax.all_gather(value_low, "seq", axis=1, tiled=True),
    )
    self_out, self_logsum = attend(query_low, key_all, value_all, self_mask)
    after_self = layer_in + linear(self_out, w_mixer) + vectors[4]
    normed_two, norm_back_two = jax.vjp(norm_rows, after_self, vectors[5], vectors[6])
    normed_two = normed_two.astype(jnp.bfloat16)
    cross_query = ((linear(normed_two, x_query) + vectors[7]) * factor).astype(jnp.bfloat16)
    frames_all = lax.all_gather(encoder_states, "seq", axis=1, tiled=True)
    cross_keys_all = linear(frames_all, x_key).astype(jnp.bfloat16)
    cross_values_all = (linear(frames_all, x_value) + vectors[8]).astype(jnp.bfloat16)
    cross_out, cross_logsum = attend(cross_query, cross_keys_all, cross_values_all, cross_mask)
    after_cross = after_self + linear(cross_out, x_mixer) + vectors[9]
    normed_three, norm_back_three = jax.vjp(norm_rows, after_cross, vectors[10], vectors[11])
    normed_three = normed_three.astype(jnp.bfloat16)
    hidden = linear(normed_three, w_expand) + vectors[12]
    gated, gate_back = jax.vjp(smooth_gate, hidden)
    gated_low = gated.astype(jnp.bfloat16)
    result = after_cross + linear(gated_low, w_reduce) + vectors[13]
    layer_output = result.astype(jnp.bfloat16)
    present = (query_pos[None, :] < lengths[:, None]).astype(jnp.float32)
    corpus_index = jnp.arange(corpus_weights.shape[0], dtype=jnp.int32)
    corpus_scale = jnp.sum(
        jnp.where(corpus_ids[:, None] == corpus_index[None, :], corpus_weights[None, :], 0.0),
        axis=1,
    )
    grad_out = cotangent.astype(jnp.float32) * (present * corpus_scale[:, None])[:, :, None]
    reduce_low = grad_out.astype(jnp.bfloat16)
    slope_reduce_bias = row_total(reduce_low)
    slope_reduce = outer_sum(gated_low, reduce_low)
    grad_hidden = gate_back(linear_back(reduce_low, w_reduce))[0]
    hidden_low = grad_hidden.astype(jnp.bfloat16)
    slope_expand_bias = row_total(hidden_low)
    slope_expand = outer_sum(normed_three, hidden_low)
    grad_norm_in, slope_gain_three, slope_bias_three = norm_back_three(
        linear_back(hidden_low, w_expand)
    )
    grad_cross = grad_out + grad_norm_in
    cross_low = grad_cross.astype(jnp.bfloat16)
    slope_xmixer_bias = row_total(cross_low)
    slope_xmixer = outer_sum(cross_out, cross_low)
    grad_heard = linear_back(cross_low, x_mixer).astype(jnp.bfloat16)
    grad_cq, part_ck, part_cv = attend_back(
        grad_heard, cross_query, cross_keys_all, cross_values_all, cross_mask, cross_logsum
    )
    slope_xkey = outer_sum(frames_all, part_ck)
    slope_xvalue = outer_sum(frames_all, part_cv)
    slope_xvalue_bias = row_total(part_cv)
    low_cq = (grad_cq * factor).astype(jnp.bfloat16)
    slope_xquery_bias = row_total(low_cq)
    slope_xquery = outer_sum(normed_two, low_cq)
    grad_norm_two, slope_gain_two, slope_bias_two = norm_back_two(linear_back(low_cq, x_query))
    grad_self = grad_cross + grad_norm_two
    self_low = grad_self.astype(jnp.bfloat16)
    slope_mixer_bias = row_total(self_low)
    slope_mixer = outer_sum(self_out, self_low)
    grad_mixed = linear_back(self_low, w_mixer).astype(jnp.bfloat16)
    grad_q, part_k, part_v = attend_back(
        grad_mixed, query_low, key_all, value_all, self_mask, self_logsum
    )
    summed_k, summed_v = (
        lax.psum_scatter(
            part_k.astype(jnp.bfloat16), "seq", scatter_dimension=1, tiled=True
        ).astype(jnp.float32),
        lax.psum_scatter(
            part_v.astype(jnp.bfloat16), "seq", scatter_dimension=1, tiled=True
        ).astype(jnp.float32),
    )
    low_k = summed_k.astype(jnp.bfloat16)
    low_v = summed_v.astype(jnp.bfloat16)
    low_q = (grad_q * factor).astype(jnp.bfloat16)
    slope_query = outer_sum(normed_one, low_q)
    slope_query_bias = row_total(low_q)
    slope_key = outer_sum(normed_one, low_k)
    slope_value = outer_sum(normed_one, low_v)
    slope_value_bias = row_total(low_v)
    grad_normed = (
        linear_back(low_q, w_query) + linear_back(low_k, w_key) + linear_back(low_v, w_value)
    )
    grad_norm_one, slope_gain_one, slope_bias_one = norm_back_one(grad_normed)
    tokens_gradient = (grad_self + grad_norm_one).astype(jnp.bfloat16)
    owned = (
        lax.psum_scatter(slope_query, "grp", scatter_dimension=0, tiled=True),
        lax.psum_scatter(slope_key, "grp", scatter_dimension=0, tiled=True),
        lax.psum_scatter(slope_value, "grp", scatter_dimension=0, tiled=True),
        lax.psum_scatter(slope_mixer, "grp", scatter_dimension=0, tiled=True),
        lax.psum_scatter(slope_xquery, "grp", scatter_dimension=0, tiled=True),
        lax.psum_scatter(slope_xkey, "grp", scatter_dimension=0, tiled=True),
        lax.psum_scatter(slope_xvalue, "grp", scatter_dimension=0, tiled=True),
        lax.psum_scatter(slope_xmixer, "grp", scatter_dimension=0, tiled=True),
        lax.psum_scatter(slope_expand, "grp", scatter_dimension=0, tiled=True),
        lax.psum_scatter(slope_reduce, "grp", scatter_dimension=0, tiled=True),
        lax.psum_scatter(slope_gain_one, "grp", scatter_dimension=0, tiled=True),
        lax.psum_scatter(slope_bias_one, "grp", scatter_dimension=0, tiled=True),
        lax.psum_scatter(slope_query_bias, "grp", scatter_dimension=0, tiled=True),
        lax.psum_scatter(slope_value_bias, "grp", scatter_dimension=0, tiled=True),
        lax.psum_scatter(slope_mixer_bias, "grp", scatter_dimension=0, tiled=True),
        lax.psum_scatter(slope_gain_two, "grp", scatter_dimension=0, tiled=True),
        lax.psum_scatter(slope_bias_two, "grp", scatter_dimension=0, tiled=True),
        lax.psum_scatter(slope_xquery_bias, "grp", scatter_dimension=0, tiled=True),
        lax.psum_scatter(slope_xvalue_bias, "grp", scatter_dimension=0, tiled=True),
        lax.psum_scatter(slope_xmixer_bias, "grp", scatter_dimension=0, tiled=True),
        lax.psum_scatter(slope_gain_three, "grp", scatter_dimension=0, tiled=True),
        lax.psum_scatter(slope_bias_three, "grp", scatter_dimension=0, tiled=True),
        lax.psum_scatter(slope_expand_bias, "grp", scatter_dimension=0, tiled=True),
        lax.psum_scatter(slope_reduce_bias, "grp", scatter_dimension=0, tiled=True),
    )
    matrices = (
        lax.psum_scatter(
            owned[0].astype(jnp.bfloat16), "seq", scatter_dimension=1, tiled=True
        ).astype(jnp.float32),
        lax.psum_scatter(
            owned[1].astype(jnp.bfloat16), "seq", scatter_dimension=1, tiled=True
        ).astype(jnp.float32),
        lax.psum_scatter(
            owned[2].astype(jnp.bfloat16), "seq", scatter_dimension=1, tiled=True
        ).astype(jnp.float32),
        lax.psum_scatter(
            owned[3].astype(jnp.bfloat16), "seq", scatter_dimension=1, tiled=True
        ).astype(jnp.float32),
        lax.psum_scatter(
            owned[4].astype(jnp.bfloat16), "seq", scatter_dimension=1, tiled=True
        ).astype(jnp.float32),
        lax.psum_scatter(
            owned[5].astype(jnp.bfloat16), "seq", scatter_dimension=1, tiled=True
        ).astype(jnp.float32),
        lax.psum_scatter(
            owned[6].astype(jnp.bfloat16), "seq", scatter_dimension=1, tiled=True
        ).astype(jnp.float32),
        lax.psum_scatter(
            owned[7].astype(jnp.bfloat16), "seq", scatter_dimension=1, tiled=True
        ).astype(jnp.float32),
        lax.psum_scatter(
            owned[8].astype(jnp.bfloat16), "seq", scatter_dimension=1, tiled=True
        ).astype(jnp.float32),
        lax.psum_scatter(
            owned[9].astype(jnp.bfloat16), "seq", scatter_dimension=1, tiled=True
        ).astype(jnp.float32),
    )
    smaller = lax.psum(
        (
            owned[10],
            owned[11],
            owned[12],
            owned[13],
            owned[14],
            owned[15],
            owned[16],
            owned[17],
            owned[18],
            owned[19],
            owned[20],
            owned[21],
            owned[22],
            owned[23],
        ),
        "seq",
    )
    return (
        layer_output,
        tokens_gradient,
        smaller[0],
        smaller[1],
        matrices[0],
        smaller[2],
        matrices[1],
        matrices[2],
        smaller[3],
        matrices[3],
        smaller[4],
        smaller[5],
        smaller[6],
        matrices[4],
        smaller[7],
        matrices[5],
        matrices[6],
        smaller[8],
        matrices[7],
        smaller[9],
        smaller[10],
        smaller[11],
        matrices[8],
        smaller[12],
        matrices[9],
        smaller[13],
    )


MESH_ID = pl.DeviceIdType.MESH
NZ, NX, NY, NC = 4, 2, 2, 2
GROUPS = 8


def where_am_i():
    grp = lax.axis_index("grp")
    seq = lax.axis_index("seq")
    return grp // NX, lax.rem(grp, NX), seq // NC, lax.rem(seq, NC)


def device_at(z, x, y, c):
    return (z * NX + x, y * NC + c)


def lanes(start, size):
    return pl.ds(pl.multiple_of(start, 128), size)


def pieces_of(bank, group, y, c, x, z_from, z_to):
    heads, mixer, pairs, wide, tall = bank
    column = pl.ds(z_from, z_to - z_from)
    if group == 0:
        return [heads.at[column, x]]
    if group == 1:
        return [mixer.at[y, column, x, :, lanes(c * 256, 256)]]
    if group < 4:
        return [pairs.at[group - 2, y, column, x, :, lanes(c * 384, 384)]]
    if group < 6:
        start = (y * NC + c) * 768 + (group - 4) * 384
        return [wide.at[column, x, :, lanes(start, 384)]]
    return [
        tall.at[y, c, pl.ds((group - 6) * 96, 96), lanes((z * NX + x) * 384, 384)]
        for z in range(z_from, z_to)
    ]


def piece_at(bank, group, y, c, x, z):
    heads, mixer, pairs, wide, tall = bank
    if group == 0:
        return heads.at[z, x]
    if group == 1:
        return mixer.at[y, z, x, :, lanes(c * 256, 256)]
    if group < 4:
        return pairs.at[group - 2, y, z, x, :, lanes(c * 384, 384)]
    if group < 6:
        return wide.at[z, x, :, lanes((y * NC + c) * 768 + (group - 4) * 384, 384)]
    return tall.at[y, c, pl.ds((group - 6) * 96, 96), lanes((z * NX + x) * 384, 384)]


def own_piece(own, group):
    heads, mixer, pairs, wide, tall = own
    if group == 0:
        return heads
    if group == 1:
        return mixer
    if group < 4:
        return pairs.at[group - 2]
    if group < 6:
        return wide.at[:, pl.ds((group - 4) * 384, 384)]
    return tall.at[pl.ds((group - 6) * 96, 96), :]


class Mail:
    def __init__(self, send_sems, recv_sems):
        self.send_sems, self.recv_sems, self.count, self.sent = send_sems, recv_sems, 0, []

    def slots(self, number):
        first = self.count
        self.count += number
        return list(range(first, first + number))

    def post(self, source, target, slot, device):
        copy = pltpu.make_async_remote_copy(
            src_ref=source,
            dst_ref=target,
            send_sem=self.send_sems.at[slot],
            recv_sem=self.recv_sems.at[slot],
            device_id=device,
            device_id_type=MESH_ID,
        )
        copy.start()
        self.sent.append(copy)

    def arrive(self, target, slot, device):
        pltpu.make_async_remote_copy(
            src_ref=target,
            dst_ref=target,
            send_sem=self.send_sems.at[slot],
            recv_sem=self.recv_sems.at[slot],
            device_id=device,
            device_id_type=MESH_ID,
        ).wait_recv()

    def finish(self):
        for copy in self.sent:
            copy.wait_send()


def greet(z, x, y, c):
    barrier = pltpu.get_barrier_semaphore()
    friends = [device_at(lax.rem(z + k, NZ), x, y, c) for k in range(1, NZ)]
    friends += [device_at(lax.rem(z + k, NZ), 1 - x, y, c) for k in range(NZ)]
    friends += [device_at(z, x, 1 - y, c), device_at(z, x, y, 1 - c), device_at(z, x, 1 - y, 1 - c)]
    for friend in friends:
        pl.semaphore_signal(barrier, inc=1, device_id=friend, device_id_type=MESH_ID)
    pl.semaphore_wait(barrier, len(friends))


def parts_in(group, number):
    return number if group >= 6 else 1


def joined(first, second):
    return jnp.concatenate([first, second], axis=1)


def mixed(first, second, core):
    even = joined(joined(first[:, :128], joined(first[:, 128:], second[:, 128:])), second[:, :128])
    odd = joined(joined(first[:, 64:], joined(second[:, :64], first[:, :64])), second[:, 64:])
    return jnp.where(core == 0, even, odd).astype(jnp.bfloat16)


def packed_heads(query, key, value, core):
    nothing = jnp.zeros_like(value[:, :64])
    even = [query[:, :128], key[:, :128], value[:, :128], query[:, 128:], key[:, 128:], value[:, 128:], nothing]
    odd = [query[:, 64:], key[:, 64:], value[:, 64:], key[:, :64], query[:, :64], nothing, value[:, :64]]
    even, odd = jnp.concatenate(even, axis=1), jnp.concatenate(odd, axis=1)
    return jnp.where(core == 0, even, odd).astype(jnp.bfloat16)


def packed_mixer(mixer, core):
    nothing = jnp.zeros_like(mixer[:, :64])
    even = joined(mixer, nothing)
    odd = joined(mixer[:, 64:], joined(nothing, mixer[:, :64]))
    return jnp.where(core == 0, even, odd).astype(jnp.bfloat16)


def own_tiles(row, y, core):
    block = jnp.where(y == 0, row[:, :384], row[:, 384:])
    lane = lax.broadcasted_iota(jnp.int32, (1, 128), 1)
    mine = lax.shift_right_logical(lane, 6) == core
    return (
        jnp.where(core == 0, block[:, :128], block[:, 256:]),
        jnp.where(mine, block[:, 128:256], jnp.zeros((1, 128), jnp.float32)),
    )


def natural_row(pair, third, y, core):
    nothing = jnp.zeros_like(pair)
    first, last = jnp.where(core == 0, pair, nothing), jnp.where(core == 0, nothing, pair)
    block = jnp.concatenate([first, third, last], axis=1)
    empty = jnp.zeros_like(block)
    return jnp.concatenate([jnp.where(y == 0, block, empty), jnp.where(y == 0, empty, block)], axis=1)


ORDER = (0, 2, 1, 3, 4, 5, 6, 7)


def forward_kernel(
    frame_span, lengths, counts,
    query_in, key_in, value_in, mixer_in, xkey_in, xvalue_in, xquery_in, xmixer_in, wide_in, tall_in,
    vectors_in, wide_bias_in, frames_short, tokens_in,
    heads, mixer, pairs, wide, tall, frames, vec_out, wide_bias,
    a_to, rows_to, third_to, o_to, h1_to, c_to, p_self_to, ck_to, cv_to, cq_to, o2_to, h2_to, m_to, p_cross_to,
    tokens_got, small, heads_here, mixer_here, pairs_here, frames_here,
    a_all, head_rows, third, o, h1, c, p_self, ck, cv, cq, o2, h2, m, p_cross,
    o_send, o_got, scores, self_scores, self_bias, cross_bias, heads_in, mixer_in_v, pairs_in, frames_in, small_in,
    send_sems, recv_sems, local_sems, load_sems, save_sems,
):
    z, x, y, c_own = where_am_i()
    heads_in[...] = packed_heads(*[ref[...].astype(jnp.float32) for ref in (query_in, key_in, value_in)], c_own)
    mixer_in_v[...] = packed_mixer(mixer_in[...].astype(jnp.float32), c_own)
    for number, (first, second) in enumerate(((xkey_in, xvalue_in), (xquery_in, xmixer_in))):
        pairs_in[number] = mixed(first[...].astype(jnp.float32), second[...].astype(jnp.float32), c_own)
    small_in[...] = jnp.zeros((32, 128), jnp.bfloat16)
    small_in[0:13, 0:96] = vectors_in[...]
    small_in[16:19, :] = wide_bias_in[...]
    frames_in[:, 368:384] = jnp.zeros((2, 16, 768), jnp.bfloat16)
    frames_in[:, 0:frame_span] = frames_short[...]
    greet(z, x, y, c_own)
    mail = Mail(send_sems, recv_sems)
    own = (heads_in, mixer_in_v, pairs_in, wide_in, tall_in)
    bank = (heads, mixer, pairs, wide, tall)
    far_mate = device_at(z, x, 1 - y, 1 - c_own)
    x_mate, y_mate = device_at(z, 1 - x, y, c_own), device_at(z, x, 1 - y, c_own)
    c_mate = device_at(z, x, y, 1 - c_own)
    z_mates = [device_at(lax.rem(z + n, NZ), x, y, c_own) for n in range(1, NZ)]
    grp = z * NX + x
    seq = y * NC + c_own

    local = []

    def keep(source, target):
        copy = pltpu.make_async_copy(source, target, local_sems.at[len(local)])
        copy.start()
        local.append(copy)

    small_slots = mail.slots(2 * NZ - 1)
    small_to = z_mates + [device_at(lax.rem(z + n, NZ), 1 - x, y, c_own) for n in range(NZ)]
    token_slots = mail.slots(3)
    frame_slots = mail.slots(3)
    z_slots = [mail.slots(NZ - 1) for _ in range(GROUPS)]
    x_slots = [mail.slots(parts_in(g, 4)) for g in range(GROUPS)]
    y_slots = [mail.slots(parts_in(g, 4)) for g in range(GROUPS)]
    dy_slots = [mail.slots(parts_in(g, VIA_X)) for g in range(GROUPS)]
    dx_slots = [mail.slots(parts_in(g, 4 - VIA_X)) for g in range(GROUPS)]
    co_slots = [mail.slots(parts_in(g, 4)) for g in range(GROUPS)]
    cx_slots = [mail.slots(parts_in(g, 4)) for g in range(GROUPS)]
    cy_slots = [mail.slots(parts_in(g, 4)) for g in range(GROUPS)]
    cdy_slots = [mail.slots(parts_in(g, VIA_X)) for g in range(GROUPS)]
    cdx_slots = [mail.slots(parts_in(g, 4 - VIA_X)) for g in range(GROUPS)]

    def to_column(group):
        for n in range(1, NZ):
            mail.post(
                own_piece(own, group), piece_at(bank, group, y, c_own, x, z), z_slots[group][n - 1], z_mates[n - 1]
            )

    def post_all(group, slots, device, yy, cc, xx, z_from, z_to):
        for slot, ref in zip(slots, pieces_of(bank, group, yy, cc, xx, z_from, z_to)):
            mail.post(ref, ref, slot, device)

    def arrive_all(group, slots, device, yy, cc, xx, z_from, z_to):
        for slot, ref in zip(slots, pieces_of(bank, group, yy, cc, xx, z_from, z_to)):
            mail.arrive(ref, slot, device)

    def spread(group):
        for n in range(1, NZ):
            zz = lax.rem(z + NZ - n, NZ)
            mail.arrive(piece_at(bank, group, y, c_own, x, zz), z_slots[group][n - 1], z_mates[n - 1])
        local[group].wait()
        post_all(group, x_slots[group], x_mate, y, c_own, x, 0, 4)
        if group == 0:
            return
        post_all(group, y_slots[group], y_mate, y, c_own, x, 0, 4)
        post_all(group, co_slots[group], c_mate, y, c_own, x, 0, 4)

    def turn(group):
        if group == 0:
            arrive_all(group, x_slots[group], x_mate, y, c_own, 1 - x, 0, 4)
            return
        arrive_all(group, y_slots[group], y_mate, 1 - y, c_own, x, 0, 4)
        post_all(group, dx_slots[group], x_mate, 1 - y, c_own, x, VIA_X, 4)
        post_all(group, cy_slots[group], c_mate, 1 - y, c_own, x, 0, 4)
        arrive_all(group, x_slots[group], x_mate, y, c_own, 1 - x, 0, 4)
        post_all(group, dy_slots[group], y_mate, y, c_own, 1 - x, 0, VIA_X)
        post_all(group, cx_slots[group], c_mate, y, c_own, 1 - x, 0, 4)

    def share(group):
        if group == 0:
            return
        arrive_all(group, dy_slots[group], y_mate, 1 - y, c_own, 1 - x, 0, VIA_X)
        post_all(group, cdy_slots[group], c_mate, 1 - y, c_own, 1 - x, 0, VIA_X)
        arrive_all(group, dx_slots[group], x_mate, 1 - y, c_own, 1 - x, VIA_X, 4)
        post_all(group, cdx_slots[group], c_mate, 1 - y, c_own, 1 - x, VIA_X, 4)

    def complete(group):
        arrive_all(group, co_slots[group], c_mate, y, 1 - c_own, x, 0, 4)
        arrive_all(group, cx_slots[group], c_mate, y, 1 - c_own, 1 - x, 0, 4)
        arrive_all(group, cy_slots[group], c_mate, 1 - y, 1 - c_own, x, 0, 4)
        arrive_all(group, cdy_slots[group], c_mate, 1 - y, 1 - c_own, 1 - x, 0, VIA_X)
        arrive_all(group, cdx_slots[group], c_mate, 1 - y, 1 - c_own, 1 - x, VIA_X, 4)

    def frame_rows(number):
        return frames.at[:, number]

    loads = []

    def load(source, target):
        copy = pltpu.make_async_copy(source, target, load_sems.at[len(loads)])
        copy.start()
        loads.append(copy)
        return copy

    def load_pair(group):
        complete(group)
        return load(pairs.at[group - 2], pairs_here.at[group - 2])

    saves = []

    def save(source, target):
        copy = pltpu.make_async_copy(source, target, save_sems.at[len(saves)])
        copy.start()
        saves.append(copy)

    for group in range(GROUPS):
        keep(own_piece(own, group), piece_at(bank, group, y, c_own, x, z))
    keep(small_in, small.at[grp])
    keep(frames_in, frame_rows(seq))
    keep(tokens_in, tokens_got.at[seq])
    to_column(ORDER[0])
    for slot, device in zip(small_slots, small_to):
        mail.post(small_in, small.at[grp], slot, device)
    to_column(ORDER[1])
    mail.post(frames_in, frame_rows(seq), frame_slots[0], y_mate)
    mail.post(frames_in, frame_rows(seq), frame_slots[1], c_mate)
    mail.post(tokens_in, tokens_got.at[seq], token_slots[0], y_mate)
    mail.post(tokens_in, tokens_got.at[seq], token_slots[1], c_mate)
    to_column(ORDER[2])

    pending = []
    for step in range(GROUPS + 2):
        if step + 3 < GROUPS:
            pending.append((to_column, ORDER[step + 3]))
        if step < GROUPS:
            pending.append((spread, ORDER[step]))
        if 0 <= step - 1 < GROUPS:
            pending.append((turn, ORDER[step - 1]))
        if 0 <= step - 2 < GROUPS:
            pending.append((share, ORDER[step - 2]))

    def tick(number=1):
        while number > 0 and pending:
            action, group = pending.pop(0)
            action(group)
            if action is not to_column:
                number -= 1

    def until(action, group):
        while (action, group) in pending:
            tick()

    for n in range(1, NZ):
        zz = lax.rem(z + NZ - n, NZ)
        mail.arrive(small.at[zz * NX + x], small_slots[n - 1], z_mates[n - 1])
    for n in range(NZ):
        zz = lax.rem(z + NZ - n, NZ)
        mail.arrive(small.at[zz * NX + 1 - x], small_slots[NZ - 1 + n], x_mate)
    local[GROUPS].wait()
    vec_out[...] = jnp.concatenate([small[g, 0:16, 0:96].astype(jnp.float32) for g in range(8)], axis=1)
    for g in range(8):
        three = small[g, 16:24, :].astype(jnp.float32)
        for n in range(3):
            at = g * 384 + n * 128
            wide_bias[:, at:at + 128] = three[n:n + 1]

    o_slots = mail.slots(6)
    until(turn, 0)
    other = (1 - y) * NC + c_own
    mail.arrive(tokens_got.at[other], token_slots[0], y_mate)
    mail.post(tokens_got.at[other], tokens_got.at[other], token_slots[2], c_mate)
    heads_loaded = load(heads, heads_here)
    mail.arrive(frame_rows(other), frame_slots[0], y_mate)
    mail.post(frame_rows(other), frame_rows(other), frame_slots[2], c_mate)
    mail.arrive(tokens_got.at[y * NC + 1 - c_own], token_slots[1], c_mate)
    mail.arrive(tokens_got.at[(1 - y) * NC + 1 - c_own], token_slots[2], c_mate)
    for copy in local[GROUPS + 1:]:
        copy.wait()
    heads_loaded.wait()
    phase = self_forward(lengths, tokens_got, vec_out, heads_here, a_all, head_rows, third, p_self, o_send, self_scores, self_bias)
    mates = ((c_mate, y * NC + 1 - c_own), (y_mate, other), (far_mate, (1 - y) * NC + 1 - c_own))
    for number, t in enumerate(phase):
        if t is not None:
            for place, (mate, mate_seq) in enumerate(mates):
                mail.post(o_send.at[mate_seq, t], o_got.at[seq, t], o_slots[3 * t + place], mate)
            o_got[seq, t] = o_send[seq, t]
        if number % 2 == 1:
            tick()
    mail.arrive(frame_rows(y * NC + 1 - c_own), frame_slots[1], c_mate)
    mail.arrive(frame_rows((1 - y) * NC + 1 - c_own), frame_slots[2], c_mate)
    frames_loaded = load(frames, frames_here)
    for source, target in ((a_all, a_to), (head_rows, rows_to), (third, third_to), (p_self, p_self_to)):
        save(source, target)
    until(share, 2)
    kv_loaded = load_pair(2)
    frames_loaded.wait()
    kv_loaded.wait()
    for number, _ in enumerate(cross_keys(frames_here, vec_out, pairs_here.at[0], ck, cv)):
        if number % 2 == 1:
            tick()
    save(ck, ck_to)
    save(cv, cv_to)
    until(share, 1)
    complete(1)
    mixer_loaded = load(mixer, mixer_here)
    for t in range(2):
        for place, (mate, mate_seq) in enumerate(mates):
            mail.arrive(o_got.at[mate_seq, t], o_slots[3 * t + place], mate)
    mixer_loaded.wait()
    self_out(tokens_got, vec_out, mixer_here, o_got, o, h1, c)
    until(share, 3)
    third_loaded = load_pair(3)
    for source, target in ((o, o_to), (h1, h1_to), (c, c_to)):
        save(source, target)
    third_loaded.wait()
    phase = cross_forward(
        counts, frame_span, c, vec_out, pairs_here.at[1], ck, cv, h1, cq, o2, h2, m, p_cross, scores, cross_bias
    )
    for number, _ in enumerate(phase):
        if 1 <= number <= 12:
            t, pair = (number - 1) // 6, (number - 1) % 6
            save(p_cross.at[t, pair], p_cross_to.at[t, pair])
        if number % 2 == 1:
            tick()
    for source, target in ((cq, cq_to), (o2, o2_to), (h2, h2_to), (m, m_to)):
        save(source, target)
    tick(100)
    for group in (4, 5, 6, 7):
        complete(group)
    for copy in saves:
        copy.wait()
    mail.finish()


VIA_X = 2


def slots_needed():
    return (2 * NZ - 1) + 12 + sum(
        3 + parts_in(g, 4) * 5 + 2 * (parts_in(g, VIA_X) + parts_in(g, 4 - VIA_X)) for g in range(GROUPS)
    )


def run_forward(lengths, counts, matrices, vectors, wide_bias, frames, tokens):
    bf16, f32 = jnp.bfloat16, jnp.float32
    number = slots_needed()
    span = tokens.shape[1]
    anywhere = pl.BlockSpec(memory_space=pl.ANY)
    inside = pl.BlockSpec(memory_space=pltpu.VMEM)
    scalar = pl.BlockSpec(memory_space=pltpu.SMEM)
    rows = (2, span, 768)
    kept = [
        ((2, 4, span, 768), bf16), ((2, 512, 640), bf16), ((2, 512, 128), bf16), (rows, bf16), (rows, f32),
        (rows, bf16), ((2, 4, 3 * span, 512), bf16), ((2, 6, 1536, 128), bf16), ((2, 6, 1536, 128), bf16), (rows, bf16),
        (rows, bf16), (rows, f32), (rows, bf16), ((2, 6, 2 * span, 1536), bf16),
    ]
    frame_span = frames.shape[1]
    frames_shape = (2, NY * NC, 384, 768)
    return pl.pallas_call(
        lambda *refs: forward_kernel(frame_span, *refs),
        out_shape=(
            jax.ShapeDtypeStruct((NZ, NX, 96, 640), bf16),
            jax.ShapeDtypeStruct((NY, NZ, NX, 96, 512), bf16),
            jax.ShapeDtypeStruct((2, NY, NZ, NX, 96, 768), bf16),
            jax.ShapeDtypeStruct((NZ, NX, 96, 3072), bf16),
            jax.ShapeDtypeStruct((NY, NC, 192, 3072), bf16),
            jax.ShapeDtypeStruct(frames_shape, bf16),
            jax.ShapeDtypeStruct((16, 768), f32),
            jax.ShapeDtypeStruct((1, 3072), f32),
        ) + tuple(jax.ShapeDtypeStruct(shape, kind) for shape, kind in kept),
        in_specs=[scalar] * 2 + [inside] * 14,
        out_specs=(anywhere,) * 6 + (inside,) * 2 + (anywhere,) * len(kept),
        scratch_shapes=[
            pltpu.VMEM((4,) + tokens.shape, bf16),
            pltpu.VMEM((8, 32, 128), bf16),
            pltpu.VMEM((NZ, NX, 96, 640), bf16),
            pltpu.VMEM((NY, NZ, NX, 96, 512), bf16),
            pltpu.VMEM((2, NY, NZ, NX, 96, 768), bf16),
            pltpu.VMEM(frames_shape, bf16),
        ] + [pltpu.VMEM(shape, kind) for shape, kind in kept] + [
            pltpu.VMEM((4, 2, span, 256), bf16),
            pltpu.VMEM((4, 2, span, 256), bf16),
            pltpu.VMEM((2 * span, 1536), f32),
            pltpu.VMEM((3 * span, 512), f32),
            pltpu.VMEM((2, 4 * span, 512), f32),
            pltpu.VMEM((2, 1, 1536), f32),
            pltpu.VMEM((96, 640), bf16),
            pltpu.VMEM((96, 256), bf16),
            pltpu.VMEM((2, 96, 384), bf16),
            pltpu.VMEM((2, 384, 768), bf16),
            pltpu.VMEM((32, 128), bf16),
            pltpu.SemaphoreType.DMA((number,)),
            pltpu.SemaphoreType.DMA((number,)),
            pltpu.SemaphoreType.DMA((GROUPS + 3,)),
            pltpu.SemaphoreType.DMA((5,)),
            pltpu.SemaphoreType.DMA((26,)),
        ],
        compiler_params=pltpu.CompilerParams(
            collective_id=1, has_side_effects=True, vmem_limit_bytes=60 << 20
        ),
        name="gather_forward",
    )(lengths, counts, *matrices, vectors, wide_bias, frames, tokens)


def mm(left, right):
    return lax.dot_general(left, right, (((1,), (0,)), ((), ())), preferred_element_type=jnp.float32)


def mm_back(left, right):
    return lax.dot_general(left, right, (((1,), (1,)), ((), ())), preferred_element_type=jnp.float32)


def mm_rows(left, right):
    return lax.dot_general(left, right, (((0,), (0,)), ((), ())), preferred_element_type=jnp.float32)


def low_lanes(rows):
    return lax.broadcasted_iota(jnp.int32, (rows, 128), 1) < 64


def turned(tile):
    return pltpu.roll(tile, 64, 1)


def tile_of(values, number):
    return values[:, number * 128:(number + 1) * 128]


def split_first(near, far):
    low = low_lanes(near.shape[0])
    return [tile_of(near, 0), jnp.where(low, tile_of(near, 1), tile_of(far, 1)), tile_of(far, 0)]


def split_second(near, far):
    low = low_lanes(near.shape[0])
    return [tile_of(near, 1), turned(jnp.where(low, tile_of(far, 0), tile_of(near, 0))), tile_of(far, 1)]


def join_first(values):
    low = low_lanes(values.shape[0])
    middle = tile_of(values, 1)
    nothing = jnp.zeros_like(middle)
    near = jnp.concatenate([tile_of(values, 0), jnp.where(low, middle, nothing)], axis=1)
    far = jnp.concatenate([tile_of(values, 2), jnp.where(low, nothing, middle)], axis=1)
    return near.astype(jnp.bfloat16), far.astype(jnp.bfloat16)


def join_second(values):
    low = low_lanes(values.shape[0])
    middle = turned(tile_of(values, 1))
    nothing = jnp.zeros_like(middle)
    near = jnp.concatenate([jnp.where(low, nothing, middle), tile_of(values, 0)], axis=1)
    far = jnp.concatenate([jnp.where(low, middle, nothing), tile_of(values, 2)], axis=1)
    return near.astype(jnp.bfloat16), far.astype(jnp.bfloat16)


def join_both(first, second):
    low = low_lanes(first.shape[0])
    mine, other = tile_of(first, 1), turned(tile_of(second, 1))
    return jnp.concatenate(
        [
            tile_of(first, 0), jnp.where(low, mine, other), tile_of(second, 0),
            tile_of(first, 2), jnp.where(low, other, mine), tile_of(second, 2),
        ],
        axis=1,
    ).astype(jnp.bfloat16)


def block_of(pair, y, at):
    if len(pair.shape) == 3:
        return pair[y, :, at]
    return pair[y, :, :, :, at].reshape(768, -1)


def times_first(values, pair):
    tiles = []
    for y in range(2):
        tiles += split_first(mm(values, block_of(pair, y, slice(0, 256))), mm(values, block_of(pair, y, slice(384, 640))))
    return tiles


def times_second(values, pair):
    tiles = []
    for y in range(2):
        tiles += split_second(mm(values, block_of(pair, y, slice(128, 384))), mm(values, block_of(pair, y, slice(512, 768))))
    return tiles


def back_first(grads, pair):
    out = None
    for y in range(2):
        near, far = join_first(grads[:, y * 384:(y + 1) * 384])
        part = mm_back(near, block_of(pair, y, slice(0, 256))) + mm_back(far, block_of(pair, y, slice(384, 640)))
        out = part if out is None else out + part
    return out


def back_second(grads, pair):
    out = None
    for y in range(2):
        near, far = join_second(grads[:, y * 384:(y + 1) * 384])
        part = mm_back(near, block_of(pair, y, slice(128, 384))) + mm_back(far, block_of(pair, y, slice(512, 768)))
        out = part if out is None else out + part
    return out


def normed(values, gain, bias):
    return norm_rows(values, gain, bias).astype(jnp.bfloat16)


def normed_back(values, gain, grads):
    centre = values - jnp.mean(values, axis=-1, keepdims=True)
    scale = lax.rsqrt(jnp.mean(centre * centre, axis=-1, keepdims=True) + EPS)
    unit = centre * scale
    inner = grads * gain
    back = scale * (
        inner - jnp.mean(inner, axis=-1, keepdims=True) - unit * jnp.mean(inner * unit, axis=-1, keepdims=True)
    )
    return back, jnp.sum(grads * unit, axis=0, keepdims=True), jnp.sum(grads, axis=0, keepdims=True)


def column_sum(values):
    return jnp.sum(values.astype(jnp.float32), axis=0, keepdims=True)


def both_heads(both):
    low = low_lanes(both.shape[0])
    nothing = jnp.zeros_like(both)
    return jnp.concatenate([jnp.where(low, both, nothing), jnp.where(low, nothing, both)], axis=0)


def stacked(values, t, pair):
    return both_heads(values[t, :, pair * 128:(pair + 1) * 128])


def third_head(tile, core):
    lane = lax.broadcasted_iota(jnp.int32, tile.shape, 1)
    return jnp.where(lax.shift_right_logical(lane, 6) == core, tile, jnp.zeros_like(tile))


def unstacked(values):
    half = values.shape[0] // 2
    return jnp.where(low_lanes(half), values[:half], values[half:])


CHUNK = 16


def soften(scores, bias, chances, rows, width):
    def one(number, carry):
        first = pl.multiple_of(number * CHUNK, CHUNK)
        values = scores[pl.ds(first, CHUNK), 0:width] + bias(first)
        raised = jnp.exp(values - jnp.max(values, axis=1, keepdims=True))
        share = raised * (1.0 / jnp.sum(raised, axis=1, keepdims=True))
        chances[pl.ds(first, CHUNK), 0:width] = share.astype(jnp.bfloat16)
        return carry

    lax.fori_loop(0, rows // CHUNK, one, 0, unroll=2 if rows // CHUNK % 2 == 0 else 3)


def soften_back(chances, slopes, grads, rows, width):
    def one(number, carry):
        first = pl.multiple_of(number * CHUNK, CHUNK)
        share = chances[pl.ds(first, CHUNK), 0:width].astype(jnp.float32)
        slope = slopes[pl.ds(first, CHUNK), 0:width]
        inner = jnp.sum(share * slope, axis=1, keepdims=True)
        grads[pl.ds(first, CHUNK), 0:width] = (share * (slope - inner)).astype(jnp.bfloat16)
        return carry

    lax.fori_loop(0, rows // CHUNK, one, 0, unroll=2 if rows // CHUNK % 2 == 0 else 3)


def self_forward(lengths, tokens, vec, heads, a_out, rows_out, third_out, p_out, o_out, scores, bias):
    span = tokens.shape[2]
    z, x, y, core = where_am_i()
    factor = 1.0 / math.sqrt(HEAD_DIM)
    for s in range(4):
        for t in range(2):
            a_out[t, s] = normed(tokens[s, t].astype(jnp.float32), vec[0:1], vec[1:2])
    yield None
    lane = lax.broadcasted_iota(jnp.int32, (1, 128), 1)
    mine = lax.shift_right_logical(lane, 6) == core
    nothing = jnp.zeros((1, 128), jnp.float32)
    query_pair, query_third = own_tiles(vec[2:3], y, core)
    value_pair, value_third = own_tiles(vec[3:4], y, core)
    offset = jnp.concatenate([query_pair, nothing, value_pair, query_third, value_third], axis=1)
    ones = nothing + 1.0
    scale = jnp.concatenate([ones * factor, ones, ones, jnp.where(mine, ones * factor, ones), ones], axis=1)
    for t in range(2):
        row = lax.broadcasted_iota(jnp.int32, (4 * span, 512), 0)
        place = lax.broadcasted_iota(jnp.int32, (4 * span, 512), 1)
        bias[t] = jnp.where((place <= row) & (place < lengths[t]), 0.0, NEG)
        product = mm(a_out[t].reshape(4 * span, 768), heads[...].reshape(768, 640))
        product = (product + offset) * scale
        rows_out[t, 0:4 * span] = product.astype(jnp.bfloat16)
        rows_out[t, 4 * span:512] = jnp.zeros((512 - 4 * span, 640), jnp.bfloat16)
        third_out[t, 0:4 * span] = turned(product[:, 384:512]).astype(jnp.bfloat16)
        third_out[t, 4 * span:512] = jnp.zeros((512 - 4 * span, 128), jnp.bfloat16)
        yield None
    for t in range(2):
        for block in range(4):
            rows, width = slice(block * span, (block + 1) * span), 128 * (block + 1)
            scores[0:2 * span, 0:width] = mm_back(
                both_heads(rows_out[t, rows, 0:128]), rows_out[t, 0:width, 128:256]
            )
            scores[2 * span:3 * span, 0:width] = mm_back(
                third_head(rows_out[t, rows, 384:512], core), third_out[t, 0:width]
            )
            chances = p_out.at[t, block]
            soften(
                scores, lambda first: bias[t, pl.ds(block * span + lax.rem(first, span), CHUNK), 0:width], chances,
                3 * span, width,
            )
            blended = mm(chances[0:2 * span, 0:width], rows_out[t, 0:width, 256:384])
            o_out[block, t, :, 0:128] = unstacked(blended).astype(jnp.bfloat16)
            blended = mm(chances[2 * span:3 * span, 0:width], rows_out[t, 0:width, 512:640])
            o_out[block, t, :, 128:256] = blended.astype(jnp.bfloat16)
            yield t if block == 3 else None


def self_out(tokens, vec, mixer, o_got, o_out, h1_out, c_out):
    span = tokens.shape[2]
    seq = lax.axis_index("seq")
    low = low_lanes(span)
    for t in range(2):
        for y in range(2):
            even, odd = o_got[2 * y, t], o_got[2 * y + 1, t]
            tiles = [even[:, 0:128], jnp.where(low, even[:, 128:256], odd[:, 128:256]), odd[:, 0:128]]
            for number, tile in enumerate(tiles):
                at = slice(y * 384 + number * 128, y * 384 + (number + 1) * 128)
                o_out[t, :, at] = tile
    rows = o_out[...].reshape(2 * span, 768)
    low = low_lanes(2 * span)
    for y in range(2):
        product = mm(rows, mixer[y].reshape(768, 512))
        tiles = [product[:, 0:128], jnp.where(low, product[:, 128:256], product[:, 384:512]), product[:, 256:384]]
        for number, tile in enumerate(tiles):
            at = slice(y * 384 + number * 128, y * 384 + (number + 1) * 128)
            for t in range(2):
                h1_out[t, :, at] = (
                    tokens[seq, t, :, at].astype(jnp.float32) + tile[t * span:(t + 1) * span] + vec[4:5, at]
                )
    for t in range(2):
        c_out[t] = normed(h1_out[t], vec[5:6], vec[6:7])


def cross_keys(frames, vec, kv, ck_out, cv_out):
    for t in range(2):
        for s in range(4):
            block = frames[t, s]
            rows = slice(s * 384, (s + 1) * 384)
            for y in range(2):
                product = mm(block, block_of(kv, y, slice(0, 768)))
                near, far = product[:, 0:384], product[:, 384:768]
                keys = split_first(near[:, 0:256], far[:, 0:256])
                values = split_second(near[:, 128:384], far[:, 128:384])
                for place in range(3):
                    at = slice(y * 384 + place * 128, y * 384 + (place + 1) * 128)
                    ck_out[t, y * 3 + place, rows] = keys[place].astype(jnp.bfloat16)
                    cv_out[t, y * 3 + place, rows] = (values[place] + vec[8:9, at]).astype(jnp.bfloat16)
            yield


def cross_forward(counts, frame_span, c, vec, xqo, ck, cv, h1, cq_out, o2_out, h2_out, m_out, p_out, scores, bias):
    span = c.shape[1]
    factor = 1.0 / math.sqrt(HEAD_DIM)
    rows = c[...].reshape(2 * span, 768)
    for number, tile in enumerate(times_first(rows, xqo)):
        at = slice(number * 128, (number + 1) * 128)
        tile = ((tile + vec[7:8, at]) * factor).astype(jnp.bfloat16)
        for t in range(2):
            cq_out[t, :, at] = tile[t * span:(t + 1) * span]
    for t in range(2):
        for s in range(4):
            inside = lax.broadcasted_iota(jnp.int32, (1, 384), 1)
            good = (inside < frame_span) & (s * frame_span + inside < counts[t])
            bias[t, :, s * 384:(s + 1) * 384] = jnp.where(good, 0.0, NEG)
    yield
    for t in range(2):
        for pair in range(6):
            at = slice(pair * 128, (pair + 1) * 128)
            scores[...] = mm_back(stacked(cq_out, t, pair), ck[t, pair])
            chances = p_out.at[t, pair]
            soften(scores, lambda first: bias[t], chances, 2 * span, 1536)
            o2_out[t, :, at] = unstacked(mm(chances[...], cv[t, pair])).astype(jnp.bfloat16)
            yield
    out = o2_out[...].reshape(2 * span, 768)
    for number, tile in enumerate(times_second(out, xqo)):
        at = slice(number * 128, (number + 1) * 128)
        for t in range(2):
            h2_out[t, :, at] = h1[t, :, at] + tile[t * span:(t + 1) * span] + vec[9:10, at]
    for t in range(2):
        m_out[t] = normed(h2_out[t], vec[10:11], vec[11:12])
    yield


class Summing:
    def __init__(self, mail, place, mates, acc, diag_x, diag_y, x_in, y_in, z_in, total):
        self.mail, self.place, self.mates = mail, place, mates
        self.acc, self.diag_x, self.diag_y = acc, diag_x, diag_y
        self.x_in, self.y_in, self.z_in, self.total = x_in, y_in, z_in, total
        self.slots = [mail.slots(4 + NZ - 1) for _ in range(acc.shape[0])]

    def begin(self, n):
        z, x, y = self.place
        x_mate, y_mate, _ = self.mates
        self.mail.post(self.acc.at[n, 1 - y, pl.ds(0, 2), 1 - x], self.diag_x.at[n], self.slots[n][0], x_mate)
        self.mail.post(self.acc.at[n, 1 - y, pl.ds(2, 2), 1 - x], self.diag_y.at[n], self.slots[n][1], y_mate)

    def side(self, n):
        z, x, y = self.place
        x_mate, y_mate, _ = self.mates
        self.mail.arrive(self.diag_x.at[n], self.slots[n][0], x_mate)
        for k in range(2):
            self.acc[n, 1 - y, k, x] = self.acc[n, 1 - y, k, x] + self.diag_x[n, k]
        self.mail.post(self.acc.at[n, 1 - y, :, x], self.y_in.at[n], self.slots[n][2], y_mate)
        self.mail.arrive(self.diag_y.at[n], self.slots[n][1], y_mate)
        for k in range(2):
            self.acc[n, y, 2 + k, 1 - x] = self.acc[n, y, 2 + k, 1 - x] + self.diag_y[n, k]
        self.mail.post(self.acc.at[n, y, :, 1 - x], self.x_in.at[n], self.slots[n][3], x_mate)

    def column(self, n):
        z, x, y = self.place
        x_mate, y_mate, z_mates = self.mates
        self.mail.arrive(self.y_in.at[n], self.slots[n][2], y_mate)
        self.mail.arrive(self.x_in.at[n], self.slots[n][3], x_mate)
        for k in range(NZ):
            self.acc[n, y, k, x] = (
                self.acc[n, y, k, x].astype(jnp.float32)
                + self.x_in[n, k].astype(jnp.float32)
                + self.y_in[n, k].astype(jnp.float32)
            ).astype(jnp.bfloat16)
        for k in range(1, NZ):
            zz = lax.rem(z + k, NZ)
            self.mail.post(self.acc.at[n, y, zz, x], self.z_in.at[n, k - 1], self.slots[n][3 + k], z_mates[k - 1])

    def last(self, n):
        z, x, y = self.place
        _, _, z_mates = self.mates
        for k in range(1, NZ):
            self.mail.arrive(self.z_in.at[n, k - 1], self.slots[n][3 + k], z_mates[k - 1])
        self.total[n] = self.acc[n, y, z, x].astype(jnp.float32) + (
            self.z_in[n, 0].astype(jnp.float32) + self.z_in[n, 1].astype(jnp.float32)
        ) + self.z_in[n, 2].astype(jnp.float32)


def summing_scratch(n, width=384):
    piece = (96, width)
    shapes = [
        (n, NY, NZ, NX) + piece, (n, 2) + piece, (n, 2) + piece, (n, NZ) + piece, (n, NZ) + piece, (n, NZ - 1) + piece
    ]
    return [pltpu.VMEM(shape, jnp.bfloat16) for shape in shapes]


class Loads:
    def __init__(self, sems):
        self.sems, self.count = sems, 0

    def start(self, source, target):
        copy = pltpu.make_async_copy(source, target, self.sems.at[self.count])
        copy.start()
        self.count += 1
        return copy


def two(first, second):
    return jnp.concatenate([first, second], axis=0)


def feed_kernel(
    lengths, ids, weights, cotangent, vec, wide_bias, h2, m, o2, c, h1, cq,
    wide_far, tall_far, pairs_far, frames_far, ck_far, cv_far, p_far,
    y_out, dh1_out, total, acc_kv, acc_xqo, small_out, wide_small,
    acc, diag_x, diag_y, x_in, y_in, z_in,
    wide, tall, xqo, frames, keys_here, values_here, p_here,
    m_sib, g_own, g_sib, du_own, du_send, du_sib, dz_own, dz_send, dz_sib,
    o2_sib, c_sib, xb_own, xb_send, xb_sib, xa_own, xa_send, xa_sib, gkv, kv_in,
    dy, dh2, do, dq, scores, dscores,
    send_sems, recv_sems, load_sems, unit_sems,
):
    z, x, y, core = where_am_i()
    span = m.shape[1]
    seq = y * NC + core
    factor = 1.0 / math.sqrt(HEAD_DIM)
    low = low_lanes(2 * span)
    x_mate, y_mate, c_mate = device_at(z, 1 - x, y, core), device_at(z, x, 1 - y, core), device_at(z, x, y, 1 - core)
    z_mates = [device_at(lax.rem(z + n, NZ), x, y, core) for n in range(1, NZ)]
    loads = Loads(load_sems)
    order = [(yy, side) for yy in range(2) for side in range(2)]
    block_loads = []
    for yy, side in order:
        at = lanes((2 * yy + (core if side == 0 else 1 - core)) * 768, 768)
        block_loads.append((
            loads.start(wide_far.at[:, :, :, at], wide.at[:, :, :, at]),
            loads.start(tall_far.at[:, :, :, at], tall.at[:, :, :, at]),
        ))
    xqo_load = loads.start(pairs_far.at[1], xqo)
    frames_load = loads.start(frames_far, frames)
    units = [(pair, t) for pair in range(6) for t in range(2)]

    def unit_copies(n):
        pair, t = units[n]
        slot = n % 2
        return [
            pltpu.make_async_copy(ck_far.at[t, pair], keys_here.at[slot], unit_sems.at[slot, 0]),
            pltpu.make_async_copy(cv_far.at[t, pair], values_here.at[slot], unit_sems.at[slot, 1]),
            pltpu.make_async_copy(p_far.at[t, pair], p_here.at[slot], unit_sems.at[slot, 2]),
        ]

    for copy in unit_copies(0):
        copy.start()
    greet(z, x, y, core)
    mail = Mail(send_sems, recv_sems)
    sums = Summing(mail, (z, x, y), (x_mate, y_mate, z_mates), acc, diag_x, diag_y, x_in, y_in, z_in, total)
    swap = mail.slots(1 + 2 + 4 + 2 + 2 + 2 + 1)
    m_slot, dz_slots, g_slots, du_slots = swap[0], swap[1:3], swap[3:7], swap[7:9]
    xb_slots, xa_slots, kv_slot = swap[9:11], swap[11:13], swap[13]
    o2_slot, c_slot = mail.slots(2)
    mail.post(m, m_sib, m_slot, c_mate)
    mail.post(o2, o2_sib, o2_slot, c_mate)
    mail.post(c, c_sib, c_slot, c_mate)

    for t in range(2):
        weight = 0.0
        for corpus in range(weights.shape[0]):
            weight = weight + jnp.where(ids[t] == corpus, weights[corpus], 0.0)
        row = lax.broadcasted_iota(jnp.int32, (span, 1), 0) + seq * span
        scale = jnp.where(row < lengths[t], weight, 0.0)
        dy[t * span:(t + 1) * span] = cotangent[t].astype(jnp.float32) * scale
    dz = dy[...].astype(jnp.bfloat16)
    dz_wide = dz.astype(jnp.float32)
    small_out[...] = jnp.zeros_like(small_out)
    small_out[12:13] = column_sum(dz_wide)
    for yy in range(2):
        tiles = [dz_wide[:, yy * 384 + n * 128:yy * 384 + (n + 1) * 128] for n in range(3)]
        even = jnp.concatenate([tiles[0], tiles[1]], axis=1)
        last = turned(tiles[2])
        odd = jnp.concatenate([jnp.where(low, turned(tiles[1]), last), last], axis=1)
        dz_own[yy] = jnp.where(core == 0, even, odd).astype(jnp.bfloat16)
        dz_send[yy] = jnp.where(core == 0, odd, even).astype(jnp.bfloat16)
        mail.post(dz_send.at[yy], dz_sib.at[yy], dz_slots[yy], c_mate)
    rows = m[...].reshape(2 * span, 768)
    z_sum, dm_sum = None, None
    for number, (yy, side) in enumerate(order):
        at = lanes((2 * yy + (core if side == 0 else 1 - core)) * 768, 768)
        for copy in block_loads[number]:
            copy.wait()
        wide_here = wide[:, :, :, at].reshape(768, 768)
        tall_here = tall[:, :, :, at].reshape(768, 768)
        hidden = mm(rows, wide_here) + wide_bias[:, at]
        bell = 0.5 * (1.0 + lax.erf(hidden * 0.7071067811865476))
        gate = (hidden * bell).astype(jnp.bfloat16)
        g_own[:, at] = gate
        mail.post(g_own.at[:, at], g_sib.at[:, at], g_slots[number], c_mate)
        slope = bell + hidden * (jnp.exp(-0.5 * hidden * hidden) * 0.3989422804014327)
        back = (mm(dz, tall_here) * slope).astype(jnp.bfloat16)
        if side == 0:
            du_own[yy] = back
        else:
            du_send[yy] = back
            mail.post(du_send.at[yy], du_sib.at[yy], du_slots[yy], c_mate)
        part = mm_back(gate, tall_here)
        z_sum = part if z_sum is None else z_sum + part
        part = mm_back(back, wide_here)
        dm_sum = part if dm_sum is None else dm_sum + part
        wide_small[:, at] = column_sum(back)
    h2_rows = h2[...].reshape(2 * span, 768)
    out = h2_rows + z_sum + vec[12:13]
    back, gain, offset = normed_back(h2_rows, vec[10:11], dm_sum)
    small_out[10:11] = gain
    small_out[11:12] = offset
    dh2[...] = dy[...] + back
    for t in range(2):
        y_out[t] = out[t * span:(t + 1) * span].astype(jnp.bfloat16)

    for number, (yy, side) in enumerate(order):
        at = lanes((2 * yy + (1 - core if side == 0 else core)) * 768, 768)
        mail.arrive(g_sib.at[:, at], g_slots[number], c_mate)
    for yy in range(2):
        mail.arrive(dz_sib.at[yy], dz_slots[yy], c_mate)
    for yy in range(2):
        slopes = two(dz_own[yy], dz_sib[yy])
        for zz in range(NZ):
            at = slice(zz * 768, (zz + 1) * 768)
            product = mm_rows(slopes, two(g_own[:, at], g_sib[:, at])).astype(jnp.bfloat16)
            for xx in range(NX):
                acc[2, yy, zz, xx] = product[0:96, xx * 384:(xx + 1) * 384]
                acc[3, yy, zz, xx] = product[96:192, xx * 384:(xx + 1) * 384]
    sums.begin(2)
    sums.begin(3)
    mail.arrive(m_sib, m_slot, c_mate)
    both_rows = two(rows, m_sib[...].reshape(2 * span, 768))
    for yy in range(2):
        mail.arrive(du_sib.at[yy], du_slots[yy], c_mate)
        product = mm_rows(both_rows, two(du_own[yy], du_sib[yy])).astype(jnp.bfloat16)
        acc[0, yy] = product[:, 0:384].reshape(NZ, NX, 96, 384)
        acc[1, yy] = product[:, 384:768].reshape(NZ, NX, 96, 384)
    sums.begin(0)
    sums.begin(1)
    pending = []
    for step in range(6):
        for lag, action in ((0, sums.side), (1, sums.column), (2, sums.last)):
            if 0 <= step - lag < 4:
                pending.append((action, (2, 3, 0, 1)[step - lag]))

    def tick(number=1):
        for _ in range(number):
            if pending:
                action, group = pending.pop(0)
                action(group)

    low_wide = dh2[...].astype(jnp.bfloat16).astype(jnp.float32)
    small_out[9:10] = column_sum(low_wide)
    xqo_load.wait()
    for yy in range(2):
        near, far = join_second(low_wide[:, yy * 384:(yy + 1) * 384])
        xb_own[yy] = jnp.where(core == 0, near, far)
        xb_send[yy] = jnp.where(core == 0, far, near)
        mail.post(xb_send.at[yy], xb_sib.at[yy], xb_slots[yy], c_mate)
    heard = back_second(low_wide, xqo)
    small_out[8:9] = column_sum(heard.astype(jnp.bfloat16))
    for t in range(2):
        do[t] = heard[t * span:(t + 1) * span].astype(jnp.bfloat16)
    tick()
    frames_load.wait()
    total_kv = None
    for number, (pair, t) in enumerate(units):
        at = slice(pair * 128, (pair + 1) * 128)
        slot = number % 2
        if number + 1 < len(units):
            for copy in unit_copies(number + 1):
                copy.start()
        for copy in unit_copies(number):
            copy.wait()
        slopes, query = stacked(do, t, pair), stacked(cq, t, pair)
        scores[...] = mm_back(slopes, values_here[slot])
        chances = p_here.at[slot]
        soften_back(chances, scores, dscores, 2 * span, 1536)
        dq[t * span:(t + 1) * span, at] = unstacked(mm(dscores[...], keys_here[slot])) * factor
        turned_grads = two(mm_rows(query, dscores[...]), mm_rows(slopes, chances[...])).astype(jnp.bfloat16)
        part = mm(turned_grads, frames[t].reshape(1536, 768))
        total_kv = part if t == 0 else total_kv + part
        if t == 1:
            keys, values = total_kv[0:128].T, total_kv[128:256].T
            yy, place = pair // 3, pair % 3
            if place == 1:
                values = turned(values)
                half = low_lanes(768)
                gkv[0, yy, :, 128:256] = jnp.where(half, keys, values).astype(jnp.bfloat16)
                gkv[1, yy, :, 128:256] = jnp.where(half, values, keys).astype(jnp.bfloat16)
            else:
                gkv[place // 2, yy, :, 0:128] = keys.astype(jnp.bfloat16)
                gkv[place // 2, yy, :, 256:384] = values.astype(jnp.bfloat16)
        tick()
    mail.post(gkv.at[1 - core], kv_in, kv_slot, c_mate)
    low_q = dq[...].astype(jnp.bfloat16).astype(jnp.float32)
    small_out[7:8] = column_sum(low_q)
    for yy in range(2):
        near, far = join_first(low_q[:, yy * 384:(yy + 1) * 384])
        xa_own[yy] = jnp.where(core == 0, near, far)
        xa_send[yy] = jnp.where(core == 0, far, near)
        mail.post(xa_send.at[yy], xa_sib.at[yy], xa_slots[yy], c_mate)
    back, gain, offset = normed_back(h1[...].reshape(2 * span, 768), vec[5:6], back_first(low_q, xqo))
    small_out[5:6] = gain
    small_out[6:7] = offset
    for t in range(2):
        dh1_out[t] = dh2[t * span:(t + 1) * span] + back[t * span:(t + 1) * span]
    mail.arrive(o2_sib, o2_slot, c_mate)
    mail.arrive(c_sib, c_slot, c_mate)
    o2_both = two(o2[...].reshape(2 * span, 768), o2_sib[...].reshape(2 * span, 768))
    c_both = two(c[...].reshape(2 * span, 768), c_sib[...].reshape(2 * span, 768))
    for yy in range(2):
        mail.arrive(xb_sib.at[yy], xb_slots[yy], c_mate)
        mail.arrive(xa_sib.at[yy], xa_slots[yy], c_mate)
        second = mm_rows(o2_both, two(xb_own[yy], xb_sib[yy]))
        first = mm_rows(c_both, two(xa_own[yy], xa_sib[yy]))
        store_pair(acc_xqo.at[yy], first, second)
    mail.arrive(kv_in, kv_slot, c_mate)
    for yy in range(2):
        acc_kv[yy] = (gkv[core, yy] + kv_in[yy]).reshape(NZ, NX, 96, 384)
    tick(100)
    mail.finish()


def store_pair(out, first, second):
    shape = (NZ, NX, 96, 128)
    out[:, :, :, 0:128] = tile_of(first, 0).astype(jnp.bfloat16).reshape(shape)
    out[:, :, :, 128:256] = (tile_of(first, 1) + tile_of(second, 0)).astype(jnp.bfloat16).reshape(shape)
    out[:, :, :, 256:384] = tile_of(second, 1).astype(jnp.bfloat16).reshape(shape)


def run_feed(lengths, ids, weights, near, far):
    bf16, f32 = jnp.bfloat16, jnp.float32
    span = near[4].shape[1]
    rows, flat = (2, span, 768), 2 * span
    inside, anywhere = pl.BlockSpec(memory_space=pltpu.VMEM), pl.BlockSpec(memory_space=pl.ANY)
    scalar = pl.BlockSpec(memory_space=pltpu.SMEM)
    piece = (NY, NZ, NX, 96, 384)
    number = 4 * 7 + 16
    scratch = [
        ((NZ, NX, 96, 3072), bf16), ((NY, NC, 192, 3072), bf16), ((NY, NZ, NX, 96, 768), bf16), (far[3].shape, bf16),
        ((2, 1536, 128), bf16), ((2, 1536, 128), bf16), ((2, flat, 1536), bf16),
        (rows, bf16), ((flat, 3072), bf16), ((flat, 3072), bf16),
        ((2, flat, 768), bf16), ((2, flat, 768), bf16), ((2, flat, 768), bf16),
        ((2, flat, 256), bf16), ((2, flat, 256), bf16), ((2, flat, 256), bf16),
        (rows, bf16), (rows, bf16),
    ] + [((2, flat, 256), bf16)] * 6 + [
        ((2, 2, 768, 384), bf16), ((2, 768, 384), bf16),
        ((flat, 768), f32), ((flat, 768), f32), (rows, bf16), ((flat, 768), f32), ((flat, 1536), f32),
        ((flat, 1536), bf16),
    ]
    return pl.pallas_call(
        feed_kernel,
        out_shape=(
            jax.ShapeDtypeStruct(rows, bf16), jax.ShapeDtypeStruct(rows, f32),
            jax.ShapeDtypeStruct((4, 96, 384), f32),
            jax.ShapeDtypeStruct(piece, bf16), jax.ShapeDtypeStruct(piece, bf16),
            jax.ShapeDtypeStruct((16, 768), f32), jax.ShapeDtypeStruct((1, 3072), f32),
        ),
        in_specs=[scalar] * 3 + [inside] * len(near) + [anywhere] * len(far),
        out_specs=(inside,) * 7,
        scratch_shapes=summing_scratch(4) + [pltpu.VMEM(shape, kind) for shape, kind in scratch] + [
            pltpu.SemaphoreType.DMA((number,)),
            pltpu.SemaphoreType.DMA((number,)),
            pltpu.SemaphoreType.DMA((10,)),
            pltpu.SemaphoreType.DMA((2, 3)),
        ],
        compiler_params=pltpu.CompilerParams(
            collective_id=2, has_side_effects=True, vmem_limit_bytes=60 << 20
        ),
        name="feed_cross_back",
    )(lengths, ids, weights, *near, *far)


def last_kernel(
    tokens, dh1, a, head_rows, third, o, p, vec, small_before, wide_small,
    heads_far, mixer_far, kv_far, xqo_far,
    dx_out, total, total_o, total_q, small_total,
    acc, diag_x, diag_y, x_in, y_in, z_in,
    acc_o, diag_x_o, diag_y_o, x_in_o, y_in_o, z_in_o,
    acc_q, x_in_q, z_in_q,
    heads, mixer, o_sib, ob_own, ob_send, ob_sib, do_send, do_got, kv_sum, dq_third, dheads,
    da_send, da_core, da_side, scores, dscores,
    small, pack, pack_in, pack_sum, pack_seq,
    send_sems, recv_sems, load_sems,
):
    z, x, y, core = where_am_i()
    span = o.shape[1]
    seq = y * NC + core
    grp = z * NX + x
    factor = 1.0 / math.sqrt(HEAD_DIM)
    x_mate, y_mate, c_mate = device_at(z, 1 - x, y, core), device_at(z, x, 1 - y, core), device_at(z, x, y, 1 - core)
    far_mate = device_at(z, x, 1 - y, 1 - core)
    z_mates = [device_at(lax.rem(z + n, NZ), x, y, core) for n in range(1, NZ)]
    loads = Loads(load_sems)
    mixer_load = loads.start(mixer_far, mixer)
    acc_loads = [loads.start(kv_far, acc.at[0]), loads.start(xqo_far, acc.at[1])]
    heads_load = loads.start(heads_far, heads)
    greet(z, x, y, core)
    mail = Mail(send_sems, recv_sems)
    mates3 = (x_mate, y_mate, z_mates)
    sums = Summing(mail, (z, x, y), mates3, acc, diag_x, diag_y, x_in, y_in, z_in, total)
    sums_o = Summing(mail, (z, x, y), mates3, acc_o, diag_x_o, diag_y_o, x_in_o, y_in_o, z_in_o, total_o)
    (o_slot,) = mail.slots(1)
    ob_slots, do_slots = mail.slots(2), mail.slots(6)
    core_slots, side_slots = mail.slots(4), mail.slots(2)
    xq_slots, zq_slots = mail.slots(2), mail.slots(6)
    pack_slots, seq_slots = mail.slots(2 * NZ - 1), mail.slots(2)
    mail.post(o, o_sib, o_slot, c_mate)
    small[...] = small_before[...]
    low_wide = dh1[...].reshape(2 * span, 768).astype(jnp.bfloat16).astype(jnp.float32)
    small[4:5] = column_sum(low_wide)
    heard = None
    mixer_load.wait()
    for yy in range(2):
        near, far = join_first(low_wide[:, yy * 384:(yy + 1) * 384])
        ob_own[yy] = jnp.where(core == 0, near, far)
        ob_send[yy] = jnp.where(core == 0, far, near)
        mail.post(ob_send.at[yy], ob_sib.at[yy], ob_slots[yy], c_mate)
        part = mm_back(jnp.concatenate([near, far], axis=1), mixer[yy].reshape(768, 512))
        heard = part if heard is None else heard + part
    for yy in range(2):
        near, far = join_first(heard[:, yy * 384:(yy + 1) * 384])
        for t in range(2):
            do_send[2 * yy, t] = near[t * span:(t + 1) * span]
            do_send[2 * yy + 1, t] = far[t * span:(t + 1) * span]
    mates = (
        (c_mate, y * NC + 1 - core), (y_mate, (1 - y) * NC + core), (far_mate, (1 - y) * NC + 1 - core)
    )
    for t in range(2):
        for place in (2, 1, 0):
            mate, mate_seq = mates[place]
            mail.post(do_send.at[mate_seq, t], do_got.at[seq, t], do_slots[3 * t + place], mate)
        do_got[seq, t] = do_send[seq, t]
    for copy in acc_loads:
        copy.wait()
    sums.begin(0)
    sums.begin(1)
    mail.arrive(o_sib, o_slot, c_mate)
    o_both = two(o[...].reshape(2 * span, 768), o_sib[...].reshape(2 * span, 768))
    for yy in range(2):
        mail.arrive(ob_sib.at[yy], ob_slots[yy], c_mate)
        product = mm_rows(o_both, two(ob_own[yy], ob_sib[yy])).astype(jnp.bfloat16)
        acc_o[0, yy] = product.reshape(NZ, NX, 96, 256)
    sums_o.begin(0)
    pending = [
        (sums.side, 0), (sums.side, 1), (sums_o.side, 0), (sums.column, 0), (sums.column, 1), (sums_o.column, 0),
        (sums.last, 0), (sums.last, 1), (sums_o.last, 0),
    ]

    def tick(number=1):
        for _ in range(number):
            if pending:
                action, group = pending.pop(0)
                action(group)

    def exchange_core(t):
        mail.post(da_send.at[y * NC + 1 - core, t], da_core.at[t, 0], core_slots[2 * t], c_mate)
        mail.post(da_send.at[(1 - y) * NC + 1 - core, t], da_core.at[t, 1], core_slots[2 * t + 1], c_mate)

    def exchange_side(t):
        mail.arrive(da_core.at[t, 1], core_slots[2 * t + 1], c_mate)
        across = (1 - y) * NC + core
        da_send[across, t] = da_send[across, t] + da_core[t, 1]
        mail.post(da_send.at[across, t], da_side.at[t], side_slots[t], y_mate)

    heads_load.wait()
    for t in range(2):
        for place, (mate, mate_seq) in enumerate(mates):
            mail.arrive(do_got.at[mate_seq, t], do_slots[3 * t + place], mate)
        for block in (3, 2, 1, 0):
            rows, width = slice(block * span, (block + 1) * span), 128 * (block + 1)
            slopes, slopes_third = both_heads(do_got[block, t, :, 0:128]), do_got[block, t, :, 128:256]
            query = both_heads(head_rows[t, rows, 0:128])
            query_third = third_head(head_rows[t, rows, 384:512], core)
            scores[0:2 * span, 0:width] = mm_back(slopes, head_rows[t, 0:width, 256:384])
            scores[2 * span:3 * span, 0:width] = mm_back(slopes_third, head_rows[t, 0:width, 512:640])
            chances = p.at[t, block]
            soften_back(chances, scores, dscores, 3 * span, width)
            pair_grads, third_grads = dscores[0:2 * span, 0:width], dscores[2 * span:3 * span, 0:width]
            dheads[t, rows, 0:128] = (
                unstacked(mm(pair_grads, head_rows[t, 0:width, 128:256])) * factor
            ).astype(jnp.bfloat16)
            dq_third[rows] = third_head(mm(third_grads, third[t, 0:width]) * factor, core)
            parts = (
                mm_rows(query, pair_grads), mm_rows(query_third, third_grads),
                mm_rows(slopes, chances[0:2 * span, 0:width]), mm_rows(slopes_third, chances[2 * span:3 * span, 0:width]),
            )
            for number, part in enumerate(parts):
                if block == 3:
                    kv_sum[number] = part
                else:
                    kv_sum[number, :, 0:width] += part
            if t == 1 and block == 3:
                exchange_side(0)
            elif (t, block) in ((0, 1), (0, 0), (1, 1), (1, 0)):
                tick()
        keys, keys_third, values, values_third = [kv_sum[number].T[0:4 * span] for number in range(4)]
        dheads[t, :, 128:256] = keys.astype(jnp.bfloat16)
        dheads[t, :, 256:384] = values.astype(jnp.bfloat16)
        dheads[t, :, 384:512] = (dq_third[...] + turned(keys_third)).astype(jnp.bfloat16)
        dheads[t, :, 512:640] = values_third.astype(jnp.bfloat16)
        if t == 1:
            inputs = two(a[0].reshape(4 * span, 768), a[1].reshape(4 * span, 768))
            product = mm_rows(inputs, two(dheads[0], dheads[1])).astype(jnp.bfloat16)
            acc_q[...] = product.reshape(NZ, NX, 96, 640)
            for part, at in enumerate((slice(0, 384), slice(384, 640))):
                mail.post(acc_q.at[:, 1 - x, :, at], x_in_q.at[:, :, at], xq_slots[part], x_mate)
        back = mm_back(dheads[t], heads[...].reshape(768, 640)).astype(jnp.bfloat16)
        for s in range(4):
            da_send[s, t] = back[s * span:(s + 1) * span]
        exchange_core(t)
    tick(2)
    exchange_side(1)
    tick()
    sums_q = [column_sum(two(dheads[0, :, n * 128:(n + 1) * 128], dheads[1, :, n * 128:(n + 1) * 128])) for n in (0, 2, 3, 4)]
    small[2:3] = natural_row(sums_q[0], third_head(sums_q[2], core), y, core)
    small[3:4] = natural_row(sums_q[1], sums_q[3], y, core)
    for part, at in enumerate((slice(0, 384), slice(384, 640))):
        mail.arrive(x_in_q.at[:, :, at], xq_slots[part], x_mate)
        for k in range(NZ):
            acc_q[k, x, :, at] = acc_q[k, x, :, at] + x_in_q[k, :, at]
        for k in range(1, NZ):
            zz = lax.rem(z + k, NZ)
            mail.post(
                acc_q.at[zz, x, :, at], z_in_q.at[k - 1, :, at], zq_slots[3 * part + k - 1], z_mates[k - 1]
            )
    gain, offset = None, None
    for t in range(2):
        mail.arrive(da_core.at[t, 0], core_slots[2 * t], c_mate)
        mail.arrive(da_side.at[t], side_slots[t], y_mate)
        back = (
            da_send[seq, t].astype(jnp.float32) + da_core[t, 0].astype(jnp.float32) + da_side[t].astype(jnp.float32)
        )
        part, gain_part, offset_part = normed_back(tokens[t].astype(jnp.float32), vec[0:1], back)
        dx_out[t] = (dh1[t] + part).astype(jnp.bfloat16)
        gain = gain_part if t == 0 else gain + gain_part
        offset = offset_part if t == 0 else offset + offset_part
    small[0:1] = gain
    small[1:2] = offset
    for g in range(8):
        pack[g, 0:16, 0:96] = small[:, g * 96:(g + 1) * 96]
        pack[g, 0:16, 96:128] = jnp.zeros((16, 32), jnp.float32)
        for n in range(3):
            at = g * 384 + n * 128
            pack[g, 16 + n:17 + n, :] = wide_small[:, at:at + 128]
        pack[g, 19:24, :] = jnp.zeros((5, 128), jnp.float32)
    pack_to = [(lax.rem(z + n, NZ), x) for n in range(1, NZ)]
    pack_to += [(lax.rem(z + n, NZ), 1 - x) for n in range(NZ)]
    for number, (zz, xx) in enumerate(pack_to):
        mail.post(pack.at[zz * NX + xx], pack_in.at[number], pack_slots[number], device_at(zz, xx, y, core))
    tick(100)
    for number in range(2 * NZ - 1):
        mail.arrive(pack_in.at[number], pack_slots[number], x_mate)
    pack_sum[...] = (
        (pack[grp] + pack_in[0]) + (pack_in[1] + pack_in[2])
        + ((pack_in[3] + pack_in[4]) + (pack_in[5] + pack_in[6]))
    )
    mail.post(pack_sum, pack_seq.at[0], seq_slots[0], c_mate)
    mail.arrive(pack_seq.at[0], seq_slots[0], c_mate)
    pack_seq[1] = pack_sum[...] + pack_seq[0]
    mail.post(pack_seq.at[1], pack_seq.at[2], seq_slots[1], y_mate)
    for part, at in enumerate((slice(0, 384), slice(384, 640))):
        for k in range(1, NZ):
            mail.arrive(z_in_q.at[k - 1, :, at], zq_slots[3 * part + k - 1], z_mates[k - 1])
        total_q[:, at] = (acc_q[z, x, :, at].astype(jnp.float32) + z_in_q[0, :, at].astype(jnp.float32)) + (
            z_in_q[1, :, at].astype(jnp.float32) + z_in_q[2, :, at].astype(jnp.float32)
        )
    mail.arrive(pack_seq.at[2], seq_slots[1], y_mate)
    small_total[...] = pack_seq[1] + pack_seq[2]
    mail.finish()


def run_last(near, far):
    bf16, f32 = jnp.bfloat16, jnp.float32
    span = near[0].shape[1]
    rows, flat = (2, span, 768), 2 * span
    inside, anywhere = pl.BlockSpec(memory_space=pltpu.VMEM), pl.BlockSpec(memory_space=pl.ANY)
    number = 3 * 7 + 1 + 2 + 6 + 6 + 8 + 9
    scratch = [
        ((NZ, NX, 96, 640), bf16), ((NZ, 96, 640), bf16), ((NZ - 1, 96, 640), bf16),
        ((NZ, NX, 96, 640), bf16), ((NY, NZ, NX, 96, 512), bf16), (rows, bf16),
        ((2, flat, 256), bf16), ((2, flat, 256), bf16), ((2, flat, 256), bf16),
        ((4, 2, span, 256), bf16), ((4, 2, span, 256), bf16), ((4, 128, 512), f32), ((4 * span, 128), f32),
        ((2, 4 * span, 640), bf16), ((4, 2, span, 768), bf16), ((2, 2, span, 768), bf16), ((2, span, 768), bf16),
        ((3 * span, 512), f32), ((3 * span, 512), bf16),
        ((16, 768), f32), ((8, 24, 128), f32), ((7, 24, 128), f32), ((24, 128), f32), ((3, 24, 128), f32),
    ]
    return pl.pallas_call(
        last_kernel,
        out_shape=(
            jax.ShapeDtypeStruct(rows, bf16), jax.ShapeDtypeStruct((2, 96, 384), f32),
            jax.ShapeDtypeStruct((1, 96, 256), f32), jax.ShapeDtypeStruct((96, 640), f32),
            jax.ShapeDtypeStruct((24, 128), f32),
        ),
        in_specs=[inside] * len(near) + [anywhere] * len(far),
        out_specs=(inside,) * 5,
        scratch_shapes=summing_scratch(2) + summing_scratch(1, 256) + [
            pltpu.VMEM(shape, kind) for shape, kind in scratch
        ] + [
            pltpu.SemaphoreType.DMA((number,)),
            pltpu.SemaphoreType.DMA((number,)),
            pltpu.SemaphoreType.DMA((4,)),
        ],
        compiler_params=pltpu.CompilerParams(
            collective_id=3, has_side_effects=True, vmem_limit_bytes=60 << 20
        ),
        name="self_back_sum",
    )(*near, *far)


def place_kernel(
    y, dx, total, total_o, total_q, total_ff, small,
    y_out, dx_out, query, key, value, mixer, xkey, xvalue, xquery, xmixer, wide, tall, *more,
):
    vectors, wide_bias = more[:13], more[13]
    core = lax.rem(lax.axis_index("seq"), NC)
    y_out[...] = y[...]
    dx_out[...] = dx[...]

    def put(out, even, odd):
        @pl.when(core == 0)
        def _():
            out[...] = jnp.concatenate(even, axis=1)

        @pl.when(core != 0)
        def _():
            out[...] = jnp.concatenate(odd, axis=1)

    heads = total_q[...]
    for out, pair, even, odd in ((query, 0, 384, 448), (key, 128, 448, 384), (value, 256, 512, 576)):
        whole = heads[:, pair:pair + 128]
        put(out, [whole, heads[:, even:even + 64]], [heads[:, odd:odd + 64], whole])
    piece = total_o[0]
    put(mixer, [piece[:, :192]], [piece[:, 192:], piece[:, :128]])
    for number, (first, second) in enumerate(((xkey, xvalue), (xquery, xmixer))):
        piece = total[number]
        put(first, [piece[:, :192]], [piece[:, 192:256], piece[:, :128]])
        put(second, [piece[:, 256:], piece[:, 192:256]], [piece[:, 128:192], piece[:, 256:]])
    wide[:, :384] = total_ff[0]
    wide[:, 384:] = total_ff[1]
    tall[:96] = total_ff[2]
    tall[96:] = total_ff[3]
    for number, out in enumerate(vectors):
        out[...] = small[number:number + 1, 0:96]
    for number in range(3):
        wide_bias[:, number * 128:(number + 1) * 128] = small[16 + number:17 + number]


def run_place(y, dx, *totals):
    f32 = jnp.float32
    inside = pl.BlockSpec(memory_space=pltpu.VMEM)
    like = jax.ShapeDtypeStruct(y.shape, y.dtype)
    return pl.pallas_call(
        place_kernel,
        out_shape=(like, like) + (jax.ShapeDtypeStruct((96, 192), f32),) * 8 + (
            jax.ShapeDtypeStruct((96, 768), f32), jax.ShapeDtypeStruct((192, 384), f32),
        ) + (jax.ShapeDtypeStruct((1, 96), f32),) * 13 + (jax.ShapeDtypeStruct((1, 384), f32),),
        in_specs=[inside] * 7,
        out_specs=(inside,) * 26,
        compiler_params=pltpu.CompilerParams(vmem_limit_bytes=60 << 20),
        name="place",
    )(y, dx, *totals)


def on_device_fast(*arguments):
    (
        tokens, encoder_states, lengths, frame_counts, corpus_ids, corpus_weights, cotangent,
        first_gain, first_bias, query_weight, query_bias, key_weight, value_weight, value_bias,
        output_weight, output_bias, second_gain, second_bias, cross_query_weight, cross_query_bias,
        cross_key_weight, cross_value_weight, cross_value_bias, cross_output_weight, cross_output_bias,
        third_gain, third_bias, expand_weight, expand_bias, reduce_weight, reduce_bias,
    ) = arguments
    bf16, f32 = jnp.bfloat16, jnp.float32
    small_vectors = (
        first_gain, first_bias, query_bias, value_bias, output_bias, second_gain, second_bias,
        cross_query_bias, cross_value_bias, cross_output_bias, third_gain, third_bias, reduce_bias, expand_bias,
    )
    matrices = (
        query_weight, key_weight, value_weight, output_weight, cross_key_weight, cross_value_weight,
        cross_query_weight, cross_output_weight, expand_weight, reduce_weight.T,
    )
    (
        heads_all, mixer_all, pairs_all, wide_all, tall_all, frames_all, vec, wide_bias,
        a_all, head_rows, third, o, h1, c, p_self, ck, cv, cq, o2, h2, m, p_cross,
    ) = run_forward(
        lengths, frame_counts, matrices, jnp.stack(small_vectors[:13]), expand_bias.reshape(3, 128), encoder_states, tokens
    )
    layer_output, dh1, total_ff, acc_kv, acc_xqo, small_before, wide_small = run_feed(
        lengths, corpus_ids, corpus_weights,
        [cotangent, vec, wide_bias, h2, m, o2, c, h1, cq],
        [wide_all, tall_all, pairs_all, frames_all, ck, cv, p_cross],
    )
    tokens_gradient, total, total_o, total_q, small_total = run_last(
        [tokens, dh1, a_all, head_rows, third, o, p_self, vec, small_before, wide_small],
        [heads_all, mixer_all, acc_kv, acc_xqo],
    )
    (
        layer_output, tokens_gradient, m_query, m_key, m_value, m_mixer, m_xkey, m_xvalue, m_xquery, m_xmixer,
        expand_grad, reduce_grad, *smaller,
    ) = run_place(layer_output, tokens_gradient, total, total_o, total_q, total_ff, small_total)
    reduce_grad = reduce_grad.T
    smaller = [row.reshape(-1) for row in smaller]
    expand_bias_grad = smaller[13]
    return (
        layer_output, tokens_gradient, smaller[0], smaller[1], m_query, smaller[2], m_key, m_value, smaller[3],
        m_mixer, smaller[4], smaller[5], smaller[6], m_xquery, smaller[7], m_xkey, m_xvalue, smaller[8],
        m_xmixer, smaller[9], smaller[10], smaller[11], expand_grad, expand_bias_grad, reduce_grad, smaller[12],
    )


def solution(mesh):
    placed = (
        P("grp", "seq", None),
        P("grp", "seq", None),
        P("grp"),
        P("grp"),
        P("grp"),
        P(),
        P("grp", "seq", None),
        P("grp"),
        P("grp"),
        P("grp", "seq"),
        P("grp"),
        P("grp", "seq"),
        P("grp", "seq"),
        P("grp"),
        P("grp", "seq"),
        P("grp"),
        P("grp"),
        P("grp"),
        P("grp", "seq"),
        P("grp"),
        P("grp", "seq"),
        P("grp", "seq"),
        P("grp"),
        P("grp", "seq"),
        P("grp"),
        P("grp"),
        P("grp"),
        P("grp", "seq"),
        P("grp"),
        P("grp", "seq"),
        P("grp"),
    )
    small_slice = mesh.shape["grp"] == NZ * NX and mesh.shape["seq"] == NY * NC
    return jax.shard_map(
        on_device_fast if small_slice else on_device_plain,
        mesh=mesh,
        in_specs=placed,
        out_specs=(
            P("grp", "seq", None),
            P("grp", "seq", None),
            P("grp"),
            P("grp"),
            P("grp", "seq"),
            P("grp"),
            P("grp", "seq"),
            P("grp", "seq"),
            P("grp"),
            P("grp", "seq"),
            P("grp"),
            P("grp"),
            P("grp"),
            P("grp", "seq"),
            P("grp"),
            P("grp", "seq"),
            P("grp", "seq"),
            P("grp"),
            P("grp", "seq"),
            P("grp"),
            P("grp"),
            P("grp"),
            P("grp", "seq"),
            P("grp"),
            P("grp", "seq"),
            P("grp"),
        ),
        check_vma=False,
    )
```

profile of v0, /device:TPU:1, one launch (start us, length us, event | category | flops | bytes accessed | tf_op | source)
XLA Modules:
  0.0 271.1 jit_solution(5959913291307223087)
XLA Ops:
  0.7 2.7 stack.55.refs_12_
  3.4 2.4 copy.57.refs_14_
  5.8 122.3 %gather_forward.1 = (bf16[4,2,96,640]{3,2,1,0:T(8,128)(2,1)}, bf16[2,4,2,96,512]{4,3,2,1,0:T(8,128)(2,1)}, bf16[2,2,4,2,96,768]{5,4,3,2,1,0:T(8,128)(2,1)}, bf16...) custom-call(s32[2]{0:T(128)} %lengths.1, ...), custom_call_target="tpu_custom_call" | custom-call | tf_op jit(solution)/shard_map/gather_forward/pallas_call | solution.py:807
  128.1 71.3 %feed_cross_back.1 = (bf16[2,112,768]{2,1,0:T(8,128)(2,1)}, f32[2,112,768]{2,1,0:T(8,128)}, f32[4,96,384]{2,1,0:T(8,128)}, bf16[2,4,2,96,384]{4,3,2,1,0:T(8,128)...) custom-call(s32[2]{0:T(128)} %lengths.1, s32[2]{0:T(128)} %ids.1, f32[9]{0:T(128)} %weights.1, ...), custom_call_target="tpu_custom_call" | custom-call | tf_op jit(solution)/shard_map/feed_cross_back/pallas_call | solution.py:1460
  199.4 66.3 %self_back_sum.1 = (bf16[2,112,768]{2,1,0:T(8,128)(2,1)}, f32[2,96,384]{2,1,0:T(8,128)}, f32[1,96,256]{2,1,0:T(8,128)}, f32[96,640]{1,0:T(8,128)}, f32[24,128]{1,0:T(8,128)}) custom-call(bf16[2,112,768]{2,1,0:T(8,128)(2,1)} %tokens.1, f32[2,112,768]{2,1,0:T(8,128)} %get-tuple-element.102.dh1, bf16[2,4,112,768]{3,2,1,0:T(8,128)(2,1)} %get-tuple-element.103.a, ...), custom_call_target="tpu_custom_call" | custom-call | tf_op jit(solution)/shard_map/self_back_sum/pallas_call | solution.py:1697
  265.7 3.6 %place.1 = (bf16[2,112,768]{2,1,0:T(8,128)(2,1)}, bf16[2,112,768]{2,1,0:T(8,128)(2,1)}, f32[96,192]{1,0:T(8,128)}, f32[96,192]{1,0:T(8,128)}, f32[96,192]{1,0:T(...) custom-call(bf16[2,112,768]{2,1,0:T(8,128)(2,1)} %get-tuple-element., ...), custom_call_target="tpu_custom_call" | custom-call | tf_op jit(solution)/shard_map/place/pallas_call | solution.py:1762
  269.3 1.3 reduce
where the time goes:
time: 276 us; the launch traced here: 271 us
  Pallas kernels  264 us (96%)
  local copies, waits for them, and re-layouts  5.08 us (2%)
    pallas_call x1, Pallas kernels, run_forward(): pl.pallas_call(lambda *refs: forward_kernel(frame_span, *refs), out_shape...  122 us
    pallas_call x1, Pallas kernels, run_feed(): pl.pallas_call(feed_kernel, out_shape=(jax.ShapeDtypeStruct(rows, bf16),...  71.3 us
    pallas_call x1, Pallas kernels, run_last(): pl.pallas_call(last_kernel, out_shape=(jax.ShapeDtypeStruct(rows, bf16),...  66.3 us

commit v1 on v0

--- a/solution.py
+++ b/solution.py
@@ -1223,7 +1223,7 @@
     wide, tall, xqo, frames, keys_here, values_here, p_here,
     m_sib, g_own, g_sib, du_own, du_send, du_sib, dz_own, dz_send, dz_sib,
     o2_sib, c_sib, xb_own, xb_send, xb_sib, xa_own, xa_send, xa_sib, gkv, kv_in,
-    dy, dh2, do, dq, scores, dscores,
+    dy, dh2, do, dq, scores, dscores, gate_slope,
     send_sems, recv_sems, load_sems, unit_sems,
 ):
     z, x, y, core = where_am_i()
@@ -1288,39 +1288,15 @@
         dz_send[yy] = jnp.where(core == 0, odd, even).astype(jnp.bfloat16)
         mail.post(dz_send.at[yy], dz_sib.at[yy], dz_slots[yy], c_mate)
     rows = m[...].reshape(2 * span, 768)
-    z_sum, dm_sum = None, None
     for number, (yy, side) in enumerate(order):
         at = lanes((2 * yy + (core if side == 0 else 1 - core)) * 768, 768)
         for copy in block_loads[number]:
             copy.wait()
-        wide_here = wide[:, :, :, at].reshape(768, 768)
-        tall_here = tall[:, :, :, at].reshape(768, 768)
-        hidden = mm(rows, wide_here) + wide_bias[:, at]
+        hidden = mm(rows, wide[:, :, :, at].reshape(768, 768)) + wide_bias[:, at]
         bell = 0.5 * (1.0 + lax.erf(hidden * 0.7071067811865476))
-        gate = (hidden * bell).astype(jnp.bfloat16)
-        g_own[:, at] = gate
+        g_own[:, at] = (hidden * bell).astype(jnp.bfloat16)
         mail.post(g_own.at[:, at], g_sib.at[:, at], g_slots[number], c_mate)
-        slope = bell + hidden * (jnp.exp(-0.5 * hidden * hidden) * 0.3989422804014327)
-        back = (mm(dz, tall_here) * slope).astype(jnp.bfloat16)
-        if side == 0:
-            du_own[yy] = back
-        else:
-            du_send[yy] = back
-            mail.post(du_send.at[yy], du_sib.at[yy], du_slots[yy], c_mate)
-        part = mm_back(gate, tall_here)
-        z_sum = part if z_sum is None else z_sum + part
-        part = mm_back(back, wide_here)
-        dm_sum = part if dm_sum is None else dm_sum + part
-        wide_small[:, at] = column_sum(back)
-    h2_rows = h2[...].reshape(2 * span, 768)
-    out = h2_rows + z_sum + vec[12:13]
-    back, gain, offset = normed_back(h2_rows, vec[10:11], dm_sum)
-    small_out[10:11] = gain
-    small_out[11:12] = offset
-    dh2[...] = dy[...] + back
-    for t in range(2):
-        y_out[t] = out[t * span:(t + 1) * span].astype(jnp.bfloat16)
-
+        gate_slope[:, at] = bell + hidden * (jnp.exp(-0.5 * hidden * hidden) * 0.3989422804014327)
     for number, (yy, side) in enumerate(order):
         at = lanes((2 * yy + (1 - core if side == 0 else core)) * 768, 768)
         mail.arrive(g_sib.at[:, at], g_slots[number], c_mate)
@@ -1336,6 +1312,22 @@
                 acc[3, yy, zz, xx] = product[96:192, xx * 384:(xx + 1) * 384]
     sums.begin(2)
     sums.begin(3)
+    z_sum, dm_sum = None, None
+    for number, (yy, side) in enumerate(order):
+        at = lanes((2 * yy + (core if side == 0 else 1 - core)) * 768, 768)
+        wide_here = wide[:, :, :, at].reshape(768, 768)
+        tall_here = tall[:, :, :, at].reshape(768, 768)
+        back = (mm(dz, tall_here) * gate_slope[:, at]).astype(jnp.bfloat16)
+        if side == 0:
+            du_own[yy] = back
+        else:
+            du_send[yy] = back
+            mail.post(du_send.at[yy], du_sib.at[yy], du_slots[yy], c_mate)
+        part = mm_back(g_own[:, at], tall_here)
+        z_sum = part if z_sum is None else z_sum + part
+        part = mm_back(back, wide_here)
+        dm_sum = part if dm_sum is None else dm_sum + part
+        wide_small[:, at] = column_sum(back)
     mail.arrive(m_sib, m_slot, c_mate)
     both_rows = two(rows, m_sib[...].reshape(2 * span, 768))
     for yy in range(2):
@@ -1345,6 +1337,15 @@
         acc[1, yy] = product[:, 384:768].reshape(NZ, NX, 96, 384)
     sums.begin(0)
     sums.begin(1)
+    h2_rows = h2[...].reshape(2 * span, 768)
+    out = h2_rows + z_sum + vec[12:13]
+    back, gain, offset = normed_back(h2_rows, vec[10:11], dm_sum)
+    small_out[10:11] = gain
+    small_out[11:12] = offset
+    dh2[...] = dy[...] + back
+    for t in range(2):
+        y_out[t] = out[t * span:(t + 1) * span].astype(jnp.bfloat16)
+
     pending = []
     for step in range(6):
         for lag, action in ((0, sums.side), (1, sums.column), (2, sums.last)):
@@ -1399,7 +1400,8 @@
             else:
                 gkv[place // 2, yy, :, 0:128] = keys.astype(jnp.bfloat16)
                 gkv[place // 2, yy, :, 256:384] = values.astype(jnp.bfloat16)
-        tick()
+        if number >= 2:
+            tick()
     mail.post(gkv.at[1 - core], kv_in, kv_slot, c_mate)
     low_q = dq[...].astype(jnp.bfloat16).astype(jnp.float32)
     small_out[7:8] = column_sum(low_q)
@@ -1455,7 +1457,7 @@
     ] + [((2, flat, 256), bf16)] * 6 + [
         ((2, 2, 768, 384), bf16), ((2, 768, 384), bf16),
         ((flat, 768), f32), ((flat, 768), f32), (rows, bf16), ((flat, 768), f32), ((flat, 1536), f32),
-        ((flat, 1536), bf16),
+        ((flat, 1536), bf16), ((flat, 3072), f32),
     ]
     return pl.pallas_call(
         feed_kernel,

time: 276 us -> 267 us (0.967)
  Pallas kernels: 264 us -> 255 us
    pallas_call x1, Pallas kernels: 71.3 us -> 61.6 us  [run_feed(): pl.pallas_call(feed_kernel, out_shape=(jax.ShapeDtypeStruct(rows, bf16),...]
where the time goes in v1:
time: 267 us; the launch traced here: 262 us
  Pallas kernels  255 us (96%)
  local copies, waits for them, and re-layouts  5.08 us (2%)
    pallas_call x1, Pallas kernels, run_forward(): pl.pallas_call(lambda *refs: forward_kernel(frame_span, *refs), out_shape...  122 us
    pallas_call x1, Pallas kernels, run_last(): pl.pallas_call(last_kernel, out_shape=(jax.ShapeDtypeStruct(rows, bf16),...  67.2 us
    pallas_call x1, Pallas kernels, run_feed(): pl.pallas_call(feed_kernel, out_shape=(jax.ShapeDtypeStruct(rows, bf16),...  61.6 us

profile of v1, /device:TPU:1, one launch (start us, length us, event | category | flops | bytes accessed | tf_op | source)
XLA Modules:
  0.0 262.3 jit_solution(4459216932277354749)
XLA Ops:
  0.7 2.7 %stack.55.refs_12_ = bf16[13,96]{1,0:T(8,128)(2,1)} concatenate(bf16[1,96]{1,0:T(2,128)(2,1)} %bitcast.31, bf16[1,96]{1,0:T(2,128)(2,1)} %bitcast.32, bf16[1,96]{1,0:T(2,128)(2,1)} %bitcast.33, bf16[1,96]{1,0:T(2,128)(2,1)} %bitcast.34, bf16[1,96]{1,0:T(2,128)(2,1)} %bitcast.35, bf16[1,96]{1,0:T(2,128)(2,1)} %bitcast.36, bf16[1,96]{1,0:T(2,128)(2,1)} %bitcast.37, ...), dimensions={0} | concatenate | bytes 4992 | tf_op jit(solution)/shard_map/stack | solution.py:1797
  3.4 2.4 copy.57.refs_14_
  5.8 122.3 %gather_forward.1 = (bf16[4,2,96,640]{3,2,1,0:T(8,128)(2,1)}, bf16[2,4,2,96,512]{4,3,2,1,0:T(8,128)(2,1)}, bf16[2,2,4,2,96,768]{5,4,3,2,1,0:T(8,128)(2,1)}, bf16...) custom-call(s32[2]{0:T(128)} %lengths.1, ...), custom_call_target="tpu_custom_call" | custom-call | tf_op jit(solution)/shard_map/gather_forward/pallas_call | solution.py:807
  128.1 61.6 %feed_cross_back.1 = (bf16[2,112,768]{2,1,0:T(8,128)(2,1)}, f32[2,112,768]{2,1,0:T(8,128)}, f32[4,96,384]{2,1,0:T(8,128)}, bf16[2,4,2,96,384]{4,3,2,1,0:T(8,128)...) custom-call(s32[2]{0:T(128)} %lengths.1, s32[2]{0:T(128)} %ids.1, f32[9]{0:T(128)} %weights.1, ...), custom_call_target="tpu_custom_call" | custom-call | tf_op jit(solution)/shard_map/feed_cross_back/pallas_call | solution.py:1462
  189.7 67.2 %self_back_sum.1 = (bf16[2,112,768]{2,1,0:T(8,128)(2,1)}, f32[2,96,384]{2,1,0:T(8,128)}, f32[1,96,256]{2,1,0:T(8,128)}, f32[96,640]{1,0:T(8,128)}, f32[24,128]{1,0:T(8,128)}) custom-call(bf16[2,112,768]{2,1,0:T(8,128)(2,1)} %tokens.1, f32[2,112,768]{2,1,0:T(8,128)} %get-tuple-element.102.dh1, bf16[2,4,112,768]{3,2,1,0:T(8,128)(2,1)} %get-tuple-element.103.a, ...), custom_call_target="tpu_custom_call" | custom-call | tf_op jit(solution)/shard_map/self_back_sum/pallas_call | solution.py:1699
  256.9 3.6 %place.1 = (bf16[2,112,768]{2,1,0:T(8,128)(2,1)}, bf16[2,112,768]{2,1,0:T(8,128)(2,1)}, f32[96,192]{1,0:T(8,128)}, f32[96,192]{1,0:T(8,128)}, f32[96,192]{1,0:T(...) custom-call(bf16[2,112,768]{2,1,0:T(8,128)(2,1)} %get-tuple-element., ...), custom_call_target="tpu_custom_call" | custom-call | tf_op jit(solution)/shard_map/place/pallas_call | solution.py:1764
  260.5 1.3 reduce

commit v2 on v1

--- a/solution.py
+++ b/solution.py
@@ -1400,7 +1400,7 @@
             else:
                 gkv[place // 2, yy, :, 0:128] = keys.astype(jnp.bfloat16)
                 gkv[place // 2, yy, :, 256:384] = values.astype(jnp.bfloat16)
-        if number >= 2:
+        if number in (2, 4, 5, 6, 7, 8, 9, 10, 11):
             tick()
     mail.post(gkv.at[1 - core], kv_in, kv_slot, c_mate)
     low_q = dq[...].astype(jnp.bfloat16).astype(jnp.float32)
@@ -1483,13 +1483,13 @@
 
 
 def last_kernel(
-    tokens, dh1, a, head_rows, third, o, p, vec, small_before, wide_small,
-    heads_far, mixer_far, kv_far, xqo_far,
+    tokens, dh1, o, vec, small_before, wide_small,
+    heads_far, mixer_far, kv_far, xqo_far, a_far, rows_far, third_far, p_far,
     dx_out, total, total_o, total_q, small_total,
     acc, diag_x, diag_y, x_in, y_in, z_in,
     acc_o, diag_x_o, diag_y_o, x_in_o, y_in_o, z_in_o,
     acc_q, x_in_q, z_in_q,
-    heads, mixer, o_sib, ob_own, ob_send, ob_sib, do_send, do_got, kv_sum, dq_third, dheads,
+    a, head_rows, third, p, heads, mixer, o_sib, ob_own, ob_send, ob_sib, do_send, do_got, kv_sum, dq_third, dheads,
     da_send, da_core, da_side, scores, dscores,
     small, pack, pack_in, pack_sum, pack_seq,
     send_sems, recv_sems, load_sems,
@@ -1505,7 +1505,9 @@
     loads = Loads(load_sems)
     mixer_load = loads.start(mixer_far, mixer)
     acc_loads = [loads.start(kv_far, acc.at[0]), loads.start(xqo_far, acc.at[1])]
+    unit_loads = [loads.start(rows_far, head_rows), loads.start(third_far, third), loads.start(p_far, p)]
     heads_load = loads.start(heads_far, heads)
+    a_load = loads.start(a_far, a)
     greet(z, x, y, core)
     mail = Mail(send_sems, recv_sems)
     mates3 = (x_mate, y_mate, z_mates)
@@ -1574,6 +1576,8 @@
         da_send[across, t] = da_send[across, t] + da_core[t, 1]
         mail.post(da_send.at[across, t], da_side.at[t], side_slots[t], y_mate)
 
+    for copy in unit_loads:
+        copy.wait()
     heads_load.wait()
     for t in range(2):
         for place, (mate, mate_seq) in enumerate(mates):
@@ -1611,6 +1615,7 @@
         dheads[t, :, 384:512] = (dq_third[...] + turned(keys_third)).astype(jnp.bfloat16)
         dheads[t, :, 512:640] = values_third.astype(jnp.bfloat16)
         if t == 1:
+            a_load.wait()
             inputs = two(a[0].reshape(4 * span, 768), a[1].reshape(4 * span, 768))
             product = mm_rows(inputs, two(dheads[0], dheads[1])).astype(jnp.bfloat16)
             acc_q[...] = product.reshape(NZ, NX, 96, 640)
@@ -1620,9 +1625,9 @@
         for s in range(4):
             da_send[s, t] = back[s * span:(s + 1) * span]
         exchange_core(t)
-    tick(2)
+    tick(1)
     exchange_side(1)
-    tick()
+    tick(1)
     sums_q = [column_sum(two(dheads[0, :, n * 128:(n + 1) * 128], dheads[1, :, n * 128:(n + 1) * 128])) for n in (0, 2, 3, 4)]
     small[2:3] = natural_row(sums_q[0], third_head(sums_q[2], core), y, core)
     small[3:4] = natural_row(sums_q[1], sums_q[3], y, core)
@@ -1689,6 +1694,7 @@
     number = 3 * 7 + 1 + 2 + 6 + 6 + 8 + 9
     scratch = [
         ((NZ, NX, 96, 640), bf16), ((NZ, 96, 640), bf16), ((NZ - 1, 96, 640), bf16),
+    ] + [(ref.shape, bf16) for ref in far[4:]] + [
         ((NZ, NX, 96, 640), bf16), ((NY, NZ, NX, 96, 512), bf16), (rows, bf16),
         ((2, flat, 256), bf16), ((2, flat, 256), bf16), ((2, flat, 256), bf16),
         ((4, 2, span, 256), bf16), ((4, 2, span, 256), bf16), ((4, 128, 512), f32), ((4 * span, 128), f32),
@@ -1710,7 +1716,7 @@
         ] + [
             pltpu.SemaphoreType.DMA((number,)),
             pltpu.SemaphoreType.DMA((number,)),
-            pltpu.SemaphoreType.DMA((4,)),
+            pltpu.SemaphoreType.DMA((8,)),
         ],
         compiler_params=pltpu.CompilerParams(
             collective_id=3, has_side_effects=True, vmem_limit_bytes=60 << 20
@@ -1802,8 +1808,8 @@
         [wide_all, tall_all, pairs_all, frames_all, ck, cv, p_cross],
     )
     tokens_gradient, total, total_o, total_q, small_total = run_last(
-        [tokens, dh1, a_all, head_rows, third, o, p_self, vec, small_before, wide_small],
-        [heads_all, mixer_all, acc_kv, acc_xqo],
+        [tokens, dh1, o, vec, small_before, wide_small],
+        [heads_all, mixer_all, acc_kv, acc_xqo, a_all, head_rows, third, p_self],
     )
     (
         layer_output, tokens_gradient, m_query, m_key, m_value, m_mixer, m_xkey, m_xvalue, m_xquery, m_xmixer,

time: 267 us -> 264 us (0.989)
  Pallas kernels: 255 us -> 252 us
where the time goes in v2:
time: 264 us; the launch traced here: 259 us
  Pallas kernels  252 us (95%)
  local copies, waits for them, and re-layouts  5.08 us (2%)
    pallas_call x1, Pallas kernels, run_forward(): pl.pallas_call(lambda *refs: forward_kernel(frame_span, *refs), out_shape...  122 us
    pallas_call x1, Pallas kernels, run_last(): pl.pallas_call(last_kernel, out_shape=(jax.ShapeDtypeStruct(rows, bf16),...  64.5 us
    pallas_call x1, Pallas kernels, run_feed(): pl.pallas_call(feed_kernel, out_shape=(jax.ShapeDtypeStruct(rows, bf16),...  61.3 us

profile of v2, /device:TPU:1, one launch (start us, length us, event | category | flops | bytes accessed | tf_op | source)
XLA Modules:
  0.0 259.3 jit_solution(9037039957719582326)
XLA Ops:
  0.7 2.7 %stack.55.refs_12_ = bf16[13,96]{1,0:T(8,128)(2,1)} concatenate(bf16[1,96]{1,0:T(2,128)(2,1)} %bitcast.31, bf16[1,96]{1,0:T(2,128)(2,1)} %bitcast.32, bf16[1,96]{1,0:T(2,128)(2,1)} %bitcast.33, bf16[1,96]{1,0:T(2,128)(2,1)} %bitcast.34, bf16[1,96]{1,0:T(2,128)(2,1)} %bitcast.35, bf16[1,96]{1,0:T(2,128)(2,1)} %bitcast.36, bf16[1,96]{1,0:T(2,128)(2,1)} %bitcast.37, ...), dimensions={0} | concatenate | bytes 4992 | tf_op jit(solution)/shard_map/stack | solution.py:1803
  3.4 2.4 copy.57.refs_14_
  5.8 122.3 %gather_forward.1 = (bf16[4,2,96,640]{3,2,1,0:T(8,128)(2,1)}, bf16[2,4,2,96,512]{4,3,2,1,0:T(8,128)(2,1)}, bf16[2,2,4,2,96,768]{5,4,3,2,1,0:T(8,128)(2,1)}, bf16...) custom-call(s32[2]{0:T(128)} %lengths.1, ...), custom_call_target="tpu_custom_call" | custom-call | tf_op jit(solution)/shard_map/gather_forward/pallas_call | solution.py:807
  128.1 61.3 %feed_cross_back.1 = (bf16[2,112,768]{2,1,0:T(8,128)(2,1)}, f32[2,112,768]{2,1,0:T(8,128)}, f32[4,96,384]{2,1,0:T(8,128)}, bf16[2,4,2,96,384]{4,3,2,1,0:T(8,128)...) custom-call(s32[2]{0:T(128)} %lengths.1, s32[2]{0:T(128)} %ids.1, f32[9]{0:T(128)} %weights.1, ...), custom_call_target="tpu_custom_call" | custom-call | tf_op jit(solution)/shard_map/feed_cross_back/pallas_call | solution.py:1462
  189.4 64.5 %self_back_sum.1 = (bf16[2,112,768]{2,1,0:T(8,128)(2,1)}, f32[2,96,384]{2,1,0:T(8,128)}, f32[1,96,256]{2,1,0:T(8,128)}, f32[96,640]{1,0:T(8,128)}, f32[24,128]{1,0:T(8,128)}) custom-call(bf16[2,112,768]{2,1,0:T(8,128)(2,1)} %tokens.1, f32[2,112,768]{2,1,0:T(8,128)} %get-tuple-element.102.dh1, bf16[2,112,768]{2,1,0:T(8,128)(2,1)} %get-tuple-element.103.o, ...), custom_call_target="tpu_custom_call" | custom-call | tf_op jit(solution)/shard_map/self_back_sum/pallas_call | solution.py:1705
  253.9 3.6 %place.1 = (bf16[2,112,768]{2,1,0:T(8,128)(2,1)}, bf16[2,112,768]{2,1,0:T(8,128)(2,1)}, f32[96,192]{1,0:T(8,128)}, f32[96,192]{1,0:T(8,128)}, f32[96,192]{1,0:T(...) custom-call(bf16[2,112,768]{2,1,0:T(8,128)(2,1)} %get-tuple-element., ...), custom_call_target="tpu_custom_call" | custom-call | tf_op jit(solution)/shard_map/place/pallas_call | solution.py:1770
  257.6 1.3 reduce

commit v3 on v2

--- a/solution.py
+++ b/solution.py
@@ -1003,7 +1003,7 @@
         chances[pl.ds(first, CHUNK), 0:width] = share.astype(jnp.bfloat16)
         return carry
 
-    lax.fori_loop(0, rows // CHUNK, one, 0, unroll=2 if rows // CHUNK % 2 == 0 else 3)
+    lax.fori_loop(0, rows // CHUNK, one, 0, unroll=7)
 
 
 def soften_back(chances, slopes, grads, rows, width):
@@ -1015,7 +1015,7 @@
         grads[pl.ds(first, CHUNK), 0:width] = (share * (slope - inner)).astype(jnp.bfloat16)
         return carry
 
-    lax.fori_loop(0, rows // CHUNK, one, 0, unroll=2 if rows // CHUNK % 2 == 0 else 3)
+    lax.fori_loop(0, rows // CHUNK, one, 0, unroll=7)
 
 
 def self_forward(lengths, tokens, vec, heads, a_out, rows_out, third_out, p_out, o_out, scores, bias):

time: 264 us -> 256 us (0.970)
  Pallas kernels: 252 us -> 244 us
    pallas_call x1, Pallas kernels: 122 us -> 116 us  [run_forward(): pl.pallas_call(lambda *refs: forward_kernel(frame_span, *refs), out_shape...]
where the time goes in v3:
time: 256 us; the launch traced here: 251 us
  Pallas kernels  244 us (95%)
  local copies, waits for them, and re-layouts  5.08 us (2%)
    pallas_call x1, Pallas kernels, run_forward(): pl.pallas_call(lambda *refs: forward_kernel(frame_span, *refs), out_shape...  116 us
    pallas_call x1, Pallas kernels, run_last(): pl.pallas_call(last_kernel, out_shape=(jax.ShapeDtypeStruct(rows, bf16),...  63.3 us
    pallas_call x1, Pallas kernels, run_feed(): pl.pallas_call(feed_kernel, out_shape=(jax.ShapeDtypeStruct(rows, bf16),...  60.7 us

profile of v3, /device:TPU:1, one launch (start us, length us, event | category | flops | bytes accessed | tf_op | source)
XLA Modules:
  0.0 251.5 jit_solution(14177287599271608398)
XLA Ops:
  0.7 2.7 %stack.55.refs_12_ = bf16[13,96]{1,0:T(8,128)(2,1)} concatenate(bf16[1,96]{1,0:T(2,128)(2,1)} %bitcast.31, bf16[1,96]{1,0:T(2,128)(2,1)} %bitcast.32, bf16[1,96]{1,0:T(2,128)(2,1)} %bitcast.33, bf16[1,96]{1,0:T(2,128)(2,1)} %bitcast.34, bf16[1,96]{1,0:T(2,128)(2,1)} %bitcast.35, bf16[1,96]{1,0:T(2,128)(2,1)} %bitcast.36, bf16[1,96]{1,0:T(2,128)(2,1)} %bitcast.37, ...), dimensions={0} | concatenate | bytes 4992 | tf_op jit(solution)/shard_map/stack | solution.py:1803
  3.4 2.4 copy.57.refs_14_
  5.8 116.3 %gather_forward.1 = (bf16[4,2,96,640]{3,2,1,0:T(8,128)(2,1)}, bf16[2,4,2,96,512]{4,3,2,1,0:T(8,128)(2,1)}, bf16[2,2,4,2,96,768]{5,4,3,2,1,0:T(8,128)(2,1)}, bf16...) custom-call(s32[2]{0:T(128)} %lengths.1, ...), custom_call_target="tpu_custom_call" | custom-call | tf_op jit(solution)/shard_map/gather_forward/pallas_call | solution.py:807
  122.0 60.7 %feed_cross_back.1 = (bf16[2,112,768]{2,1,0:T(8,128)(2,1)}, f32[2,112,768]{2,1,0:T(8,128)}, f32[4,96,384]{2,1,0:T(8,128)}, bf16[2,4,2,96,384]{4,3,2,1,0:T(8,128)...) custom-call(s32[2]{0:T(128)} %lengths.1, s32[2]{0:T(128)} %ids.1, f32[9]{0:T(128)} %weights.1, ...), custom_call_target="tpu_custom_call" | custom-call | tf_op jit(solution)/shard_map/feed_cross_back/pallas_call | solution.py:1462
  182.8 63.3 %self_back_sum.1 = (bf16[2,112,768]{2,1,0:T(8,128)(2,1)}, f32[2,96,384]{2,1,0:T(8,128)}, f32[1,96,256]{2,1,0:T(8,128)}, f32[96,640]{1,0:T(8,128)}, f32[24,128]{1,0:T(8,128)}) custom-call(bf16[2,112,768]{2,1,0:T(8,128)(2,1)} %tokens.1, f32[2,112,768]{2,1,0:T(8,128)} %get-tuple-element.102.dh1, bf16[2,112,768]{2,1,0:T(8,128)(2,1)} %get-tuple-element.103.o, ...), custom_call_target="tpu_custom_call" | custom-call | tf_op jit(solution)/shard_map/self_back_sum/pallas_call | solution.py:1705
  246.1 3.6 %place.1 = (bf16[2,112,768]{2,1,0:T(8,128)(2,1)}, bf16[2,112,768]{2,1,0:T(8,128)(2,1)}, f32[96,192]{1,0:T(8,128)}, f32[96,192]{1,0:T(8,128)}, f32[96,192]{1,0:T(...) custom-call(bf16[2,112,768]{2,1,0:T(8,128)(2,1)} %get-tuple-element., ...), custom_call_target="tpu_custom_call" | custom-call | tf_op jit(solution)/shard_map/place/pallas_call | solution.py:1770
  249.7 1.3 reduce
